TPU v7x, 32 devices: a whole 2x2x4 slice. The times are simulated.
32 devices in a mesh: wide: 8 (over z, x), narrow: 4 (over y, core).
Axes of the slice: x: 2, y: 2, z: 4, core: 2. Of those that a mesh axis runs over, the one named last changes fastest.
Arguments:
- block_input: bfloat16 [64, 2048, 1024], P(('wide', 'narrow')), may hold values from -6 to 6
- query_weight: bfloat16 [1024, 1024], P('wide'), may hold values from -0.1875 to 0.1875
- key_weight: bfloat16 [1024, 1024], P('wide'), may hold values from -0.1875 to 0.1875
- value_weight: bfloat16 [1024, 1024], P('wide'), may hold values from -0.1875 to 0.1875
- out_weight: bfloat16 [1024, 1024], P('wide'), may hold values from -0.75 to 0.75
- up_weight: bfloat16 [1024, 4096], P('wide'), may hold values from -0.1875 to 0.1875
- down_weight: bfloat16 [4096, 1024], P('wide'), may hold values from -0.09375 to 0.09375
- attn_gain: bfloat16 [1024], P('wide'), may hold values from 0.099609375 to 1.8984375
- mlp_gain: bfloat16 [1024], P('wide'), may hold values from 0.099609375 to 1.8984375
- router_weight: bfloat16 [1024], replicated, may hold values from -0.1875 to 0.1875
- slots: int32 [64, 256], P(('wide', 'narrow')), may hold values from 0 to 2047, as said below
- segments: int32 [64, 2048], P(('wide', 'narrow')), may hold values from 0 to 7, never falling along the last dimension, each value on 1 to 512 neighbouring positions
- pad_mask: int32 [64, 2048], P(('wide', 'narrow')), may hold values from 0 to 1, as said below
- cotangent: bfloat16 [64, 2048, 1024], P(('wide', 'narrow')), may hold values from -6 to 6
Outputs:
- block_output: bfloat16 [64, 2048, 1024], P(('wide', 'narrow'))
- input_grad: bfloat16 [64, 2048, 1024], P(('wide', 'narrow'))
- grad_query: float32 [1024, 1024], P('wide')
- grad_key: float32 [1024, 1024], P('wide')
- grad_value: float32 [1024, 1024], P('wide')
- grad_out: float32 [1024, 1024], P('wide')
- grad_up: float32 [1024, 4096], P('wide')
- grad_down: float32 [4096, 1024], P('wide')
- grad_attn_gain: float32 [1024], P('wide')
- grad_mlp_gain: float32 [1024], P('wide')
- grad_router: float32 [1024], replicated
- statistics: float32 [2], replicated
Inputs may be any that keep to these rules, and one draw needn't show every extreme that they name: `slots`: each row holds 256 different positions in increasing order, each where pad_mask is 1. `pad_mask`: in each row the ones come first, then the zeros, with more than 256 ones.
All inputs are finite; a program needn't handle non-finite values.
Results may differ from a plain program's by a relative error of at most 0.012.
Values may be sent and summed in bfloat16 or wider, within the bound.
A program may use at most 256 MiB of HBM per device.

v0:
```python
import math

import jax
import jax.numpy as jnp
from jax import lax
from jax.sharding import PartitionSpec as P

HEADS = 16
HEAD_DIM = 64


def rms_gain(values, gain):
    return values * lax.rsqrt(jnp.mean(values * values, axis=-1, keepdims=True) + 1e-06) * gain


def attention_logits(queries, keys, allowed, scale):
    logits = (
        jnp.einsum("sqhe,skhe->shqk", queries, keys, preferred_element_type=jnp.float32) * scale
    )
    return jnp.where(allowed[:, None], logits, -1e30)


def body(
    block_input,
    query_weight,
    key_weight,
    value_weight,
    out_weight,
    up_weight,
    down_weight,
    attn_gain,
    mlp_gain,
    router_weight,
    slots,
    segments,
    pad_mask,
    cotangent,
):
    seq_count, seq_len, width = block_input.shape
    capacity = slots.shape[1]
    routed_rows = seq_count * capacity
    scale = 1.0 / math.sqrt(HEAD_DIM)
    f32 = jnp.float32
    bf16 = jnp.bfloat16
    w_query, w_key, w_value, w_out, w_up, w_down, gain_one, gain_two = (
        lax.all_gather(query_weight, "wide", axis=0, tiled=True),
        lax.all_gather(key_weight, "wide", axis=0, tiled=True),
        lax.all_gather(value_weight, "wide", axis=0, tiled=True),
        lax.all_gather(out_weight, "wide", axis=0, tiled=True),
        lax.all_gather(up_weight, "wide", axis=0, tiled=True),
        lax.all_gather(down_weight, "wide", axis=0, tiled=True),
        lax.all_gather(attn_gain, "wide", axis=0, tiled=True),
        lax.all_gather(mlp_gain, "wide", axis=0, tiled=True),
    )
    gain_attn = gain_one.astype(f32)
    gain_mlp = gain_two.astype(f32)
    routed = jnp.take_along_axis(block_input, slots[:, :, None], axis=1).reshape(routed_rows, width)
    routed_f = routed.astype(f32)
    router_gate = jax.nn.sigmoid(jnp.dot(routed, router_weight, preferred_element_type=f32))
    mask_f = pad_mask.astype(f32)
    all_logits = jnp.einsum("std,d->st", block_input, router_weight, preferred_element_type=f32)
    chosen_local = jnp.sum(jnp.take_along_axis(mask_f, slots, axis=1))
    valid_local = jnp.sum(mask_f)
    gate_local = jnp.sum(mask_f * jax.nn.sigmoid(all_logits))
    chosen_total, valid_total, gate_total = lax.psum(
        (chosen_local, valid_local, gate_local), ("wide", "narrow")
    )
    normed_one = rms_gain(routed_f, gain_attn).astype(bf16)
    head_shape = (seq_count, capacity, HEADS, HEAD_DIM)
    queries = (
        jnp.dot(normed_one, w_query, preferred_element_type=f32).astype(bf16).reshape(head_shape)
    )
    keys = jnp.dot(normed_one, w_key, preferred_element_type=f32).astype(bf16).reshape(head_shape)
    values = (
        jnp.dot(normed_one, w_value, preferred_element_type=f32).astype(bf16).reshape(head_shape)
    )
    slot_segs = jnp.take_along_axis(segments, slots, axis=1)
    order = jnp.arange(capacity, dtype=jnp.int32)
    allowed = (order[:, None] >= order[None, :])[None] & (
        slot_segs[:, :, None] == slot_segs[:, None, :]
    )
    logits = attention_logits(queries, keys, allowed, scale)
    log_total = jax.nn.logsumexp(logits, axis=-1, keepdims=True)
    probs = jnp.exp(logits - log_total).astype(bf16)
    mixed = (
        jnp.einsum("shqk,skhe->sqhe", probs, values, preferred_element_type=f32)
        .reshape(routed_rows, width)
        .astype(bf16)
    )
    attn_out = jnp.dot(mixed, w_out, preferred_element_type=f32)
    resid = routed_f + attn_out
    normed_two = rms_gain(resid, gain_mlp).astype(bf16)
    pre_act = jnp.dot(normed_two, w_up, preferred_element_type=f32)
    activ = jax.nn.gelu(pre_act).astype(bf16)
    mlp_out = jnp.dot(activ, w_down, preferred_element_type=f32)
    branch = attn_out + mlp_out
    new_rows = (
        (routed_f + router_gate[:, None] * branch).astype(bf16).reshape(seq_count, capacity, width)
    )
    seq_ids = jnp.arange(seq_count, dtype=jnp.int32)[:, None]
    block_output = block_input.at[seq_ids, slots].set(new_rows)
    w_query, w_key, w_value, w_out, w_up, w_down, gain_one, gain_two = (
        lax.all_gather(query_weight, "wide", axis=0, tiled=True),
        lax.all_gather(key_weight, "wide", axis=0, tiled=True),
        lax.all_gather(value_weight, "wide", axis=0, tiled=True),
        lax.all_gather(out_weight, "wide", axis=0, tiled=True),
        lax.all_gather(up_weight, "wide", axis=0, tiled=True),
        lax.all_gather(down_weight, "wide", axis=0, tiled=True),
        lax.all_gather(attn_gain, "wide", axis=0, tiled=True),
        lax.all_gather(mlp_gain, "wide", axis=0, tiled=True),
    )
    gain_attn = gain_one.astype(f32)
    gain_mlp = gain_two.astype(f32)
    out_grad = (
        jnp.take_along_axis(cotangent, slots[:, :, None], axis=1)
        .reshape(routed_rows, width)
        .astype(f32)
    )
    branch_grad = router_gate[:, None] * out_grad
    logit_grad = jnp.sum(out_grad * branch, axis=-1) * router_gate * (1.0 - router_gate)
    mlp_grad = branch_grad.astype(bf16)
    grad_down = jnp.einsum("tf,td->fd", activ, mlp_grad, preferred_element_type=f32)
    activ_grad = jnp.einsum("td,fd->tf", mlp_grad, w_down, preferred_element_type=f32)
    unused_act, gelu_back = jax.vjp(jax.nn.gelu, pre_act)
    pre_grad = gelu_back(activ_grad)[0].astype(bf16)
    grad_up = jnp.einsum("td,tf->df", normed_two, pre_grad, preferred_element_type=f32)
    normed_two_grad = jnp.einsum("tf,df->td", pre_grad, w_up, preferred_element_type=f32)
    unused_two, norm_two_back = jax.vjp(rms_gain, resid, gain_mlp)
    resid_grad, gain_mlp_grad = norm_two_back(normed_two_grad)
    attn_grad = (branch_grad + resid_grad).astype(bf16)
    grad_out = jnp.einsum("te,td->ed", mixed, attn_grad, preferred_element_type=f32)
    mixed_grad = (
        jnp.einsum("td,ed->te", attn_grad, w_out, preferred_element_type=f32)
        .astype(bf16)
        .reshape(head_shape)
    )
    probs_full = jnp.exp(attention_logits(queries, keys, allowed, scale) - log_total)
    prob_grad = jnp.einsum("sqhe,skhe->shqk", mixed_grad, values, preferred_element_type=f32)
    logit_grads = (
        probs_full * (prob_grad - jnp.sum(probs_full * prob_grad, axis=-1, keepdims=True))
    ).astype(bf16)
    query_grad = (
        (jnp.einsum("shqk,skhe->sqhe", logit_grads, keys, preferred_element_type=f32) * scale)
        .astype(bf16)
        .reshape(routed_rows, width)
    )
    key_grad = (
        (jnp.einsum("shqk,sqhe->skhe", logit_grads, queries, preferred_element_type=f32) * scale)
        .astype(bf16)
        .reshape(routed_rows, width)
    )
    value_grad = (
        jnp.einsum("shqk,sqhe->skhe", probs, mixed_grad, preferred_element_type=f32)
        .astype(bf16)
        .reshape(routed_rows, width)
    )
    grad_query = jnp.einsum("td,te->de", normed_one, query_grad, preferred_element_type=f32)
    grad_key = jnp.einsum("td,te->de", normed_one, key_grad, preferred_element_type=f32)
    grad_value = jnp.einsum("td,te->de", normed_one, value_grad, preferred_element_type=f32)
    normed_one_grad = jnp.einsum("te,de->td", query_grad, w_query, preferred_element_type=f32)
    normed_one_grad = normed_one_grad + jnp.einsum(
        "te,de->td", key_grad, w_key, preferred_element_type=f32
    )
    normed_one_grad = normed_one_grad + jnp.einsum(
        "te,de->td", value_grad, w_value, preferred_element_type=f32
    )
    unused_one, norm_one_back = jax.vjp(rms_gain, routed_f, gain_attn)
    routed_norm_grad, gain_attn_grad = norm_one_back(normed_one_grad)
    routed_grad = (
        out_grad + resid_grad + routed_norm_grad + logit_grad[:, None] * router_weight.astype(f32)
    )
    input_grad = cotangent.at[seq_ids, slots].set(
        routed_grad.astype(bf16).reshape(seq_count, capacity, width)
    )
    router_local = jnp.dot(logit_grad, routed_f, precision=lax.Precision.HIGHEST)
    (
        share_query,
        share_key,
        share_value,
        share_out,
        share_up,
        share_down,
        share_gain_one,
        share_gain_two,
    ) = (
        lax.psum_scatter(grad_query, "wide", scatter_dimension=0, tiled=True),
        lax.psum_scatter(grad_key, "wide", scatter_dimension=0, tiled=True),
        lax.psum_scatter(grad_value, "wide", scatter_dimension=0, tiled=True),
        lax.psum_scatter(grad_out, "wide", scatter_dimension=0, tiled=True),
        lax.psum_scatter(grad_up, "wide", scatter_dimension=0, tiled=True),
        lax.psum_scatter(grad_down, "wide", scatter_dimension=0, tiled=True),
        lax.psum_scatter(gain_attn_grad, "wide", scatter_dimension=0, tiled=True),
        lax.psum_scatter(gain_mlp_grad, "wide", scatter_dimension=0, tiled=True),
    )
    (
        total_query,
        total_key,
        total_value,
        total_out,
        total_up,
        total_down,
        total_gain_one,
        total_gain_two,
    ) = lax.psum(
        (
            share_query,
            share_key,
            share_value,
            share_out,
            share_up,
            share_down,
            share_gain_one,
            share_gain_two,
        ),
        "narrow",
    )
    router_total = lax.psum(router_local, ("wide", "narrow"))
    statistics = jnp.stack([chosen_total / valid_total, gate_total / valid_total])
    return (
        block_output,
        input_grad,
        total_query,
        total_key,
        total_value,
        total_out,
        total_up,
        total_down,
        total_gain_one,
        total_gain_two,
        router_total,
        statistics,
    )


def solution(mesh):
    return jax.shard_map(
        body,
        mesh=mesh,
        in_specs=(
            P(("wide", "narrow"), None, None),
            P("wide", None),
            P("wide", None),
            P("wide", None),
            P("wide", None),
            P("wide", None),
            P("wide", None),
            P("wide"),
            P("wide"),
            P(),
            P(("wide", "narrow"), None),
            P(("wide", "narrow"), None),
            P(("wide", "narrow"), None),
            P(("wide", "narrow"), None, None),
        ),
        out_specs=(
            P(("wide", "narrow"), None, None),
            P(("wide", "narrow"), None, None),
            P("wide", None),
            P("wide", None),
            P("wide", None),
            P("wide", None),
            P("wide", None),
            P("wide", None),
            P("wide"),
            P("wide"),
            P(),
            P(),
        ),
        check_vma=False,
    )
```

profile of v0, /device:TPU:0, one launch (start us, length us, event | category | flops | bytes accessed | tf_op | source)
XLA Modules:
  0.0 1732.4 jit_solution(7248909200291625049)
XLA Ops:
  7.2 7.8 copy.112
  15.0 7.8 copy.113
  26.7 8.2 gather_fusion.2
  35.4 22.2 %all-gather = bf16[8,1,128]{2,1,0:T(2,128)(2,1)S(1)} all-gather(bf16[1,1,128]{2,1,0:T(2,128)(2,1)S(1)} %bitcast.186), channel_id=1, replica_groups=mesh['wide'=8,'narrow'=4] {'wide'}, dimensions={0}, use_global_device_ids=true | all-gather | bytes 2304 | tf_op jit(solution)/shard_map/all_gather | solution.py:52
  62.6 8.2 gather_fusion.3
  70.8 16.3 all-gather.1
  100.9 24.0 %all-gather.13.cloned.1.call-done = bf16[1024,1024]{1,0:T(8,128)(2,1)} async-done(((bf16[128,1024]{1,0:T(8,128)(2,1)}), bf16[1024,1024]{1,0:T(8,128)(2,1)}) %all-gather.13.cloned.1.call-update) | async-done | bytes 2097168 | tf_op jit(solution)/shard_map/all_gather | solution.py:47
  133.2 41.7 %all-gather.9.cloned.1.call-done = bf16[1024,1024]{1,0:T(8,128)(2,1)} async-done(((bf16[128,1024]{1,0:T(8,128)(2,1)}), bf16[1024,1024]{1,0:T(8,128)(2,1)}) %all-gather.9.cloned.1.call-update) | async-done | bytes 2097168 | tf_op jit(solution)/shard_map/all_gather | solution.py:48
  197.1 27.5 %all-gather.15.cloned.1.call-done = bf16[1024,1024]{1,0:T(8,128)(2,1)} async-done(((bf16[128,1024]{1,0:T(8,128)(2,1)}), bf16[1024,1024]{1,0:T(8,128)(2,1)}) %all-gather.15.cloned.1.call-update) | async-done | bytes 2097168 | tf_op jit(solution)/shard_map/all_gather | solution.py:49
  224.6 5.2 multiply_reduce_fusion.3
  229.8 120.2 %all-gather.19.cloned.1.call-done = bf16[4096,1024]{1,0:T(8,128)(2,1)} async-done(((bf16[512,1024]{1,0:T(8,128)(2,1)}), bf16[4096,1024]{1,0:T(8,128)(2,1)}) %all-gather.19.cloned.1.call-update) | async-done | bytes 8388624 | tf_op jit(solution)/shard_map/all_gather | solution.py:51
  350.0 11.5 fusion.51
  361.5 113.6 %all-gather.17.cloned.1.call-done = bf16[1024,4096]{1,0:T(8,128)(2,1)} async-done(((bf16[128,4096]{1,0:T(8,128)(2,1)}), bf16[1024,4096]{1,0:T(8,128)(2,1)}) %all-gather.17.cloned.1.call-update) | async-done | bytes 8388624 | tf_op jit(solution)/shard_map/all_gather | solution.py:50
  475.2 18.9 %fusion.6 = (bf16[512,4096]{1,0:T(8,128)(2,1)}, f32[512,4096]{1,0:T(8,128)}) fusion(f32[512,4096]{1,0:T(8,128)} %fusion.51, bf16[1024,4096]{1,0:T(8,128)(2,1)} %all-gather.17.cloned.1.call-done, f32[512,1024]{1,0:T(8,128)} %get-tuple-element.34, f32[1024]{0:T(1024)S(1)} %bitcast.180, f32[512]{0:T(512)S(1)} %fusion.39), kind=kOutput, calls=%fused_computation.14 | convolution fusion | flops 4338483200 | bytes 31463424 | tf_op jit(solution)/shard_map/dot_general | solution.py:93
  494.0 8.7 multiply_reduce_fusion.1
  502.8 10.3 fusion.22
  524.2 6.8 multiply_reduce_fusion
  558.5 5.4 fusion.26
  568.6 13.4 fusion.47
  582.5 15.4 fusion.49
  605.4 23.6 %reduce-scatter.9.cloned.1.call-done = f32[128,1024]{1,0:T(8,128)} async-done(((f32[1024,1024]{1,0:T(8,128)}), f32[128,1024]{1,0:T(8,128)}) %reduce-scatter.9.cloned.1.call-update) | async-done | bytes 524304 | tf_op jit(solution)/shard_map/reduce_scatter | solution.py:187
  629.0 91.7 %reduce-scatter.7.cloned.1.call-done = f32[128,1024]{1,0:T(8,128)} async-done(((f32[1024,1024]{1,0:T(8,128)}), f32[128,1024]{1,0:T(8,128)}) %reduce-scatter.7.cloned.1.call-update) | async-done | bytes 524304 | tf_op jit(solution)/shard_map/reduce_scatter | solution.py:186
  720.7 91.4 %reduce-scatter.13.cloned.1.call-done = f32[128,1024]{1,0:T(8,128)} async-done(((f32[1024,1024]{1,0:T(8,128)}), f32[128,1024]{1,0:T(8,128)}) %reduce-scatter.13.cloned.1.call-update) | async-done | bytes 524304 | tf_op jit(solution)/shard_map/reduce_scatter | solution.py:189
  812.1 91.8 %reduce-scatter.11.cloned.1.call-done = f32[128,1024]{1,0:T(8,128)} async-done(((f32[1024,1024]{1,0:T(8,128)}), f32[128,1024]{1,0:T(8,128)}) %reduce-scatter.11.cloned.1.call-update) | async-done | bytes 524304 | tf_op jit(solution)/shard_map/reduce_scatter | solution.py:188
  903.8 286.3 %reduce-scatter.15.cloned.1.call-done = f32[128,4096]{1,0:T(8,128)} async-done(((f32[1024,4096]{1,0:T(8,128)}), f32[128,4096]{1,0:T(8,128)}) %reduce-scatter.15.cloned.1.call-update) | async-done | bytes 2097168 | tf_op jit(solution)/shard_map/reduce_scatter | solution.py:190
  1190.1 285.8 %reduce-scatter.17.cloned.1.call-done = f32[512,1024]{1,0:T(8,128)} async-done(((f32[4096,1024]{1,0:T(8,128)}), f32[512,1024]{1,0:T(8,128)}) %reduce-scatter.17.cloned.1.call-update) | async-done | bytes 2097168 | tf_op jit(solution)/shard_map/reduce_scatter | solution.py:191
  1476.0 5.6 fusion.59
  1482.8 40.3 %all-reduce.2 = (f32[1024]{0:T(1024)}, f32[]{:T(128)}, f32[]{:T(128)}, f32[]{:T(128)}) all-reduce(f32[1024]{0:T(1024)S(1)} %bitcast.185, f32[]{:T(128)} %get-tuple-element.18, f32[]{:T(128)} %get-tuple-element.17, f32[]{:T(128)} %select_reduce_fusion), channel_id=1, replica_groups=mesh['wide'=8,'narrow'=4] {'wide','narrow'}, use_global_device_ids=true, to_apply=%region_28.30 | all-reduce | flops 1027 | bytes 8216 | tf_op jit(solution)/shard_map/psum | solution.py:217
  1534.0 21.4 %all-reduce.3 = (f32[1024]{0:T(1024)S(1)}, f32[1024]{0:T(1024)S(1)}) all-reduce(f32[1024]{0:T(1024)S(1)} %get-tuple-element.15, f32[1024]{0:T(1024)S(1)} %get-tuple-element.13), channel_id=8, replica_groups=mesh['wide'=8,'narrow'=4] {'wide'}, use_global_device_ids=true, to_apply=%region_23.25.clone | all-reduce | flops 2048 | bytes 16384
  1559.1 74.9 %scatter_fusion.1 = bf16[2,2048,1024]{2,1,0:T(8,128)(2,1)} fusion(bf16[2,2048,1024]{2,1,0:T(8,128)(2,1)} %copy.113, s32[512]{0:T(512)S(1)} %bitcast.146, bf16[512,1024]{1,0:T(8,128)(2,1)S(1)} %fusion.21), kind=kCustom, calls=%fused_computation.5 | custom fusion | bytes 3149824 | tf_op jit(solution)/shard_map/scatter | solution.py:172
  1634.0 74.5 %scatter_fusion = bf16[2,2048,1024]{2,1,0:T(8,128)(2,1)} fusion(bf16[2,2048,1024]{2,1,0:T(8,128)(2,1)} %copy.112, s32[512]{0:T(512)S(1)} %bitcast.147, bf16[512,1024]{1,0:T(8,128)(2,1)S(1)} %copy-done.15), kind=kCustom, calls=%fused_computation.4 | custom fusion | bytes 3149824 | tf_op jit(solution)/shard_map/scatter | solution.py:101
  1708.5 6.2 all-reduce.4
  (189 shorter events, 127.8 us)
Async XLA Ops:
  7.2 50.5 %copy-start = (s32[2,2048]{1,0:T(2,128)S(1)}, s32[2,2048]{1,0:T(2,128)}, u32[]{:S(2)}) copy-start(s32[2,2048]{1,0:T(2,128)} %param.27) | copy-start | bytes 49156
  7.2 84.6 %all-gather.11.cloned.1.call-start = ((), (), s32[]{:S(2)}) async-start(), calls=%async_computation.7 | async-start | bytes 2359296 | tf_op jit(solution)/shard_map/all_gather | solution.py:46
  15.0 11.1 copy-start.25
  22.8 102.1 %all-gather.13.cloned.1.call-start = ((), (), s32[]{:S(2)}) async-start(), calls=%async_computation.8 | async-start | bytes 2359296 | tf_op jit(solution)/shard_map/all_gather | solution.py:47
  23.5 151.3 %all-gather.9.cloned.1.call-start = ((), (), s32[]{:S(2)}) async-start(), calls=%async_computation.6 | async-start | bytes 2359296 | tf_op jit(solution)/shard_map/all_gather | solution.py:48
  24.3 200.3 %all-gather.15.cloned.1.call-start = ((), (), s32[]{:S(2)}) async-start(), calls=%async_computation.9 | async-start | bytes 2359296 | tf_op jit(solution)/shard_map/all_gather | solution.py:49
  24.9 325.2 %all-gather.19.cloned.1.call-start = ((), (), s32[]{:S(2)}) async-start(), calls=%async_computation.11 | async-start | bytes 9437184 | tf_op jit(solution)/shard_map/all_gather | solution.py:51
  25.4 449.7 %all-gather.17.cloned.1.call-start = ((), (), s32[]{:S(2)}) async-start(), calls=%async_computation.10 | async-start | bytes 9437184 | tf_op jit(solution)/shard_map/all_gather | solution.py:50
  26.0 603.0 %reduce-scatter.9.cloned.1.call-start = ((), (), s32[]{:S(2)}) async-start(), calls=%async_computation.13 | async-start | bytes 4718592 | tf_op jit(solution)/shard_map/reduce_scatter | solution.py:187
  26.7 8.8 copy-start.34
  34.9 27.7 %copy-start.30 = (bf16[1024]{0:T(1024)(128)(2,1)S(1)}, bf16[1024]{0:T(1024)(128)(2,1)}, u32[]{:S(2)}) copy-start(bf16[1024]{0:T(1024)(128)(2,1)} %param.25) | copy-start | bytes 6148
  35.4 35.4 %copy-start.31 = (f32[1,2,2,128]{3,1,2,0:T(2,128)}, f32[1,2,2,128]{3,1,2,0:T(2,128)S(1)}, u32[]{:S(2)}) copy-start(f32[1,2,2,128]{3,1,2,0:T(2,128)S(1)} %copy.93) | copy-start | bytes 6148
  35.4 53.8 %copy-start.26 = (f32[512]{0:T(512)}, f32[512]{0:T(512)S(1)}, u32[]{:S(2)}) copy-start(f32[512]{0:T(512)S(1)} %rsqrt.25) | copy-start | bytes 6148
  57.6 32.9 %copy-start.22 = (f32[8,1,128]{2,1,0:T(1,128)}, f32[8,1,128]{2,1,0:T(1,128)S(1)}, u32[]{:S(2)}) copy-start(f32[8,1,128]{2,1,0:T(1,128)S(1)} %convert_element_type.139) | copy-start | bytes 12292
  62.5 8.3 copy-start.35
  475.2 18.9 %copy-start.5 = (f32[512,1024]{1,0:T(8,128)S(1)}, f32[512,1024]{1,0:T(8,128)}, u32[]{:S(2)}) copy-start(f32[512,1024]{1,0:T(8,128)} %get-tuple-element.34) | copy-start | bytes 6291460
  494.0 8.7 copy-start.11
  494.0 8.7 copy-start.36
  502.7 10.4 copy-start.9
  502.8 11.3 copy-start.10
  542.7 178.0 %reduce-scatter.7.cloned.1.call-start = ((), (), s32[]{:S(2)}) async-start(), calls=%async_computation.12 | async-start | bytes 4718592 | tf_op jit(solution)/shard_map/reduce_scatter | solution.py:186
  551.5 260.6 %reduce-scatter.13.cloned.1.call-start = ((), (), s32[]{:S(2)}) async-start(), calls=%async_computation.15 | async-start | bytes 4718592 | tf_op jit(solution)/shard_map/reduce_scatter | solution.py:189
  557.3 346.6 %reduce-scatter.11.cloned.1.call-start = ((), (), s32[]{:S(2)}) async-start(), calls=%async_computation.14 | async-start | bytes 4718592 | tf_op jit(solution)/shard_map/reduce_scatter | solution.py:188
  568.6 621.6 %reduce-scatter.15.cloned.1.call-start = ((), (), s32[]{:S(2)}) async-start(), calls=%async_computation.16 | async-start | bytes 18874368 | tf_op jit(solution)/shard_map/reduce_scatter | solution.py:190
  582.0 893.9 %reduce-scatter.17.cloned.1.call-start = ((), (), s32[]{:S(2)}) async-start(), calls=%async_computation.17 | async-start | bytes 18874368 | tf_op jit(solution)/shard_map/reduce_scatter | solution.py:191
  597.9 5.6 copy-start.38
  597.9 1117.4 %all-reduce.8.cloned.1.call-start = ((), (), s32[]{:S(2)}) async-start(), calls=%async_computation.18 | async-start | bytes 12582912 | tf_op jit(solution)/shard_map/psum | solution.py:204
  1476.0 6.3 copy-start.29
  1530.9 24.7 %copy-start.32 = (f32[1,2,2,128]{3,1,2,0:T(2,128)S(1)}, f32[1,2,2,128]{3,1,2,0:T(2,128)}, u32[]{:S(2)}) copy-start(f32[1,2,2,128]{3,1,2,0:T(2,128)} %copy-done.31) | copy-start | bytes 6148
  1559.1 74.9 %copy-start.15 = (bf16[512,1024]{1,0:T(8,128)(2,1)S(1)}, bf16[512,1024]{1,0:T(8,128)(2,1)}, u32[]{:S(2)}) copy-start(bf16[512,1024]{1,0:T(8,128)(2,1)} %get-tuple-element.38) | copy-start | bytes 3145732
  1715.3 7.7 copy-start.13
  1715.3 9.0 copy-start.12
  (21 other events, 56.4 us)
Sparse Core Ops, SparseCore 0:
  22.9 51.9 all-gather.10
  77.1 47.7 all-gather.12
  127.0 47.7 all-gather.8
  176.8 47.7 all-gather.14
  226.6 123.4 all-gather.18
  352.0 123.1 all-gather.16
  542.8 86.1 reduce-scatter.8
  633.0 87.6 reduce-scatter.6
  724.4 87.6 reduce-scatter.12
  816.0 87.7 reduce-scatter.10
  907.6 282.4 reduce-scatter.14
  1194.3 281.6 reduce-scatter.16
  1478.7 120.9 all-reduce.7
where the time goes:
time: 1740 us; the launch traced here: 1730 us
  waiting for transfers between devices  1200 us (69%)
  local copies, waits for them, and re-layouts  242 us (14%)
  matrix products  146 us (8%)
  blocking collectives  106 us (6%)
  between operations  18.1 us (1%)
    reduce_scatter x1, waiting for transfers between devices, body(): lax.psum_scatter(grad_up, 'wide', scatter_dimension=0, tiled=True)  286 us
    reduce_scatter x1, waiting for transfers between devices, body(): lax.psum_scatter(grad_down, 'wide', scatter_dimension=0, tiled=True)  286 us
    all_gather x1, waiting for transfers between devices, body(): lax.all_gather(down_weight, 'wide', axis=0, tiled=True)  120 us
    all_gather x1, waiting for transfers between devices, body(): lax.all_gather(up_weight, 'wide', axis=0, tiled=True)  114 us
    reduce_scatter x1, waiting for transfers between devices, body(): lax.psum_scatter(grad_value, 'wide', scatter_dimension=0, tiled=True)  91.8 us
    reduce_scatter x1, waiting for transfers between devices, body(): lax.psum_scatter(grad_query, 'wide', scatter_dimension=0, tiled=True)  91.7 us
    reduce_scatter x1, waiting for transfers between devices, body(): lax.psum_scatter(grad_out, 'wide', scatter_dimension=0, tiled=True)  91.4 us
    scatter x1, local copies, waits for them, and re-layouts, body(): cotangent.at[seq_ids, slots]  74.9 us
  transfers between devices with their start and end apart: 13, of which 11 were waited for; matrix products, arithmetic and copies ran while one was open for 18% of the time, Pallas kernels for 0%

commit v1 on v0

v1 whole, which is shorter than its diff:
```python
import functools
import math

import jax
import jax.numpy as jnp
from jax import lax
from jax.experimental import pallas as pl
from jax.experimental.pallas import tpu as pltpu
from jax.sharding import PartitionSpec as P

HEADS = 16
HEAD_DIM = 64
EPS = 1e-06
LANES = 128
MESH = pl.DeviceIdType.MESH
f32 = jnp.float32
bf16 = jnp.bfloat16
MIB = 2**20
CHUNK = 512
DEBUG = ()


def dot(a, b, ca, cb):
    return lax.dot_general(a, b, (((ca,), (cb,)), ((), ())), preferred_element_type=f32)


def aligned(start, size):
    return pl.ds(pl.multiple_of(start, size), size)


def loop(count, step):
    def run(i, carry):
        step(i)
        return carry

    lax.fori_loop(0, count, run, 0)


class Links:
    def __init__(self, send, recv):
        self.send, self.recv, self.count, self.open = send, recv, 0, []

    def make(self, src, dst, device):
        i = self.count
        self.count += 1
        return pltpu.make_async_remote_copy(
            src_ref=src,
            dst_ref=dst,
            send_sem=self.send.at[i],
            recv_sem=self.recv.at[i],
            device_id=device,
            device_id_type=MESH,
        )

    def go(self, src, dst, device):
        copy = self.make(src, dst, device)
        copy.start()
        self.open.append(copy)
        return copy

    def sent(self, copy):
        copy.wait_send()
        self.open = [other for other in self.open if other is not copy]

    def sent_all(self, copies):
        for copy in copies:
            self.sent(copy)

    def drain(self):
        for copy in self.open:
            copy.wait_send()
        self.open = []


def copy_count(far):
    near = far - 1
    gather = 2 * (8 * near + 2) + 3 * (2 * near + 1)
    narrow = 2 * 6 + 2 * 3
    reduce_mlp = 2 * (far + near + 3)
    reduce_attn = 4 * (1 + 2 * far + near + 3)
    return gather + narrow + reduce_mlp + reduce_attn + 3 + near


def block_kernel(dims, names, *refs):
    r = dict(zip(names, refs))
    A, R, T, S, CAP, SEQ, D, RB = (
        dims[k] for k in ("A", "R", "T", "S", "CAP", "SEQ", "D", "RB")
    )
    Wd = 2 * A
    half, quart = D // 2, D // 4
    scale = 1.0 / math.sqrt(HEAD_DIM)
    w, n = lax.axis_index("wide"), lax.axis_index("narrow")
    z, x = w // 2, w % 2
    y, c = n // 2, n % 2
    WA, WU, WD, GP = r["WA"], r["WU"], r["WD"], r["GP"]
    NT, MG, ACT, DG = r["NT"], r["MG"], r["ACT"], r["DG"]
    QKVM, N1, RT, OG = r["QKVM"], r["N1"], r["RT"], r["OG"]
    AO, NG, MO = r["AO"], r["NG"], r["MO"]
    PS, PR, YS, YR = r["PS"], r["PR"], r["YS"], r["YR"]
    GATE, R1, R2, LG = r["GATE"], r["R1"], r["R2"], r["LG"]
    SEGC, SEGR, STAT, SM = r["SEGC"], r["SEGR"], r["STAT"], r["SM"]
    local, credit = r["local"], r["credit"]
    links = Links(r["send"], r["recv"])

    def dev(zz, xx, yy, cc):
        return (zz * 2 + xx, yy * 2 + cc)

    to_x, to_y, to_c = dev(z, 1 - x, y, c), dev(z, x, 1 - y, c), dev(z, x, y, 1 - c)
    ahead = [(z + dz) % A for dz in range(A)]
    behind = [(z - dz + A) % A for dz in range(A)]

    own = [
        pltpu.make_async_copy(r["w_query"], WA.at[0, w], local.at[0]),
        pltpu.make_async_copy(r["w_key"], WA.at[1, w], local.at[1]),
        pltpu.make_async_copy(r["w_value"], WA.at[2, w], local.at[2]),
        pltpu.make_async_copy(r["w_out"], WA.at[3, w], local.at[3]),
        pltpu.make_async_copy(r["w_up"], WU.at[z, x], local.at[4]),
        pltpu.make_async_copy(r["w_down"].at[aligned(n * R, R)], WD.at[z, x], local.at[5]),
        pltpu.make_async_copy(r["gains"], GP.at[w], local.at[6]),
    ]
    for copy in own:
        copy.start()
    fetches = {}

    def fetch(i, slot):
        s, k = i // (SEQ // CHUNK), i % (SEQ // CHUNK)
        return [
            pltpu.make_async_copy(
                r[name].at[s, aligned(k * CHUNK, CHUNK)], QKVM.at[2 * slot + a], local.at[7 + 2 * slot + a]
            )
            for a, name in enumerate(("block_input", "cotangent"))
        ]

    for copy in fetch(0, 0):
        copy.start()
    barrier = pltpu.get_barrier_semaphore()
    peers = [dev(ahead[dz], x, y, c) for dz in range(1, A)] + [to_x, to_y, to_c]
    for peer in peers:
        pl.semaphore_signal(barrier, inc=1, device_id=peer, device_id_type=MESH)
    pl.semaphore_wait(barrier, len(peers))
    for copy in own:
        copy.wait()

    class AttnGather:
        def __init__(self, first, count):
            self.first, self.count = first, count

        def piece(self, zz, xx, yy):
            return WA.at[pl.ds(self.first, self.count), zz * 2 + xx, :, aligned(c * half + yy * quart, quart)]

        def wide_piece(self, zz, xx):
            return WA.at[pl.ds(self.first, self.count), zz * 2 + xx, :, aligned(c * half, half)]

        def start(self):
            p, q = self.piece(z, x, y), self.wide_piece(z, x)
            self.far = {dz: links.go(p, p, dev(ahead[dz], x, y, c)) for dz in range(1, A)}
            self.x0 = links.go(q, q, to_x)
            self.x1, self.y1, self.second, self.core = {}, {}, {}, []

        def to_core(self, p):
            self.core.append(links.go(p, p, to_c))

        def relay(self, dz):
            self.far[dz].wait_recv()
            p = self.piece(behind[dz], x, y)
            self.x1[dz] = links.go(p, p, to_x)
            self.y1[dz] = links.go(p, p, to_y)
            self.to_core(p)

        def relay_own(self):
            self.x0.wait_recv()
            self.to_core(self.wide_piece(z, 1 - x))

        def relay_second(self, dz):
            self.x1[dz].wait_recv()
            p = self.piece(behind[dz], 1 - x, y)
            if dz % 2:
                self.second[dz] = links.go(p, p, to_y)
            self.to_core(p)
            self.y1[dz].wait_recv()
            p = self.piece(behind[dz], x, 1 - y)
            if not dz % 2:
                self.second[dz] = links.go(p, p, to_x)
            self.to_core(p)

        def relay_third(self, dz):
            self.second[dz].wait_recv()
            self.to_core(self.piece(behind[dz], 1 - x, 1 - y))

        def finish(self):
            for copy in self.core:
                copy.wait_recv()

    class WideGather:
        def __init__(self, at):
            self.at = at

        def start(self):
            p = self.at(z, x)
            self.far = {dz: links.go(p, p, dev(ahead[dz], x, y, c)) for dz in range(1, A)}
            self.near = [links.go(p, p, to_x)]

        def relay(self, dz):
            self.far[dz].wait_recv()
            p = self.at(behind[dz], x)
            self.near.append(links.go(p, p, to_x))

        def finish(self):
            for copy in self.near:
                copy.wait_recv()

        def release(self):
            links.sent_all(list(self.far.values()) + self.near)

    gains = WideGather(lambda zz, xx: GP.at[zz * 2 + xx])
    qkv, out = AttnGather(0, 3), AttnGather(3, 1)
    up = WideGather(lambda zz, xx: WU.at[zz, xx])
    down = WideGather(lambda zz, xx: WD.at[zz, xx])
    gains.start()
    qkv.start()
    out.start()

    AO[...] = jnp.zeros_like(AO)
    NG[...] = jnp.zeros_like(NG)
    SEGC[...] = jnp.zeros_like(SEGC)
    SEGR[...] = jnp.zeros_like(SEGR)
    STAT[...] = jnp.zeros_like(STAT)
    steps = S * (SEQ // CHUNK)

    def gather_step(i):
        slot = i % 2
        s, k = i // (SEQ // CHUNK), i % (SEQ // CHUNK)

        @pl.when(i + 1 < steps)
        def _():
            for copy in fetch(i + 1, (i + 1) % 2):
                copy.start()

        for copy in fetch(i, slot):
            copy.wait()
        position = lax.broadcasted_iota(jnp.int32, (CAP, CHUNK), 1) + k * CHUNK
        onehot = jnp.where(r["slots"][s] == position, 1.0, 0.0).astype(bf16)
        rows = aligned(s * CAP, CAP)
        tokens = QKVM[2 * slot]
        AO[rows, :] += dot(onehot, tokens, 1, 0)
        NG[rows, :] += dot(onehot, QKVM[2 * slot + 1], 1, 0)
        marks = r["marks"][s, :, aligned(k * CHUNK, CHUNK)]
        mask = marks[1:2].astype(f32)
        gate_logits = dot(r["router"][...], tokens, 1, 1)[0:1]
        STAT[0:1] += mask * jax.nn.sigmoid(gate_logits)
        STAT[1:2] += mask
        SEGR[s] += dot(marks, onehot, 1, 1)
        SEGC[s] += dot(onehot, jnp.broadcast_to(marks[0:1].astype(f32), (LANES, CHUNK)).astype(bf16), 1, 1)

    loop(steps, gather_step)

    step_rows = T // 4
    router_row = r["router"][0:1].astype(f32)

    def gate_step(i):
        rows = aligned(i * step_rows, step_rows)
        v, g = AO[rows, :], NG[rows, :]
        gate = jax.nn.sigmoid(jnp.sum(v * router_row, axis=-1, keepdims=True))
        GATE[rows, :] = gate
        R1[rows, :] = lax.rsqrt(jnp.mean(v * v, axis=-1, keepdims=True) + EPS)
        RT[rows, :] = v.astype(bf16)
        OG[rows, :] = g.astype(bf16)
        MG[n, rows, :] = (gate * g).astype(bf16)

    loop(4, gate_step)

    class RowShare:
        def __init__(self, at):
            self.at = at

        def start(self, k):
            p = self.at(n, k)
            self.core = getattr(self, "core", {})
            self.far = getattr(self, "far", {})
            self.core[k] = links.go(p, p, to_c)
            self.far[k] = links.go(p, p, to_y)

        def relay(self, k):
            self.far[k].wait_recv()
            p = self.at((1 - y) * 2 + c, k)
            self.last = getattr(self, "last", {})
            self.last[k] = links.go(p, p, to_c)

        def release(self):
            for copies in (self.core, self.far, self.last):
                links.sent_all(list(copies.values()))

    rows_half = T // 2
    share_mg = RowShare(lambda b, k: MG.at[b, pl.ds(k * rows_half, rows_half)])
    share_nt = RowShare(lambda b, k: NT.at[b, pl.ds(k * (A // 2), A // 2)])

    for dz in range(1, A):
        gains.relay(dz)
    for dz in range(1, A):
        qkv.relay(dz)
    up.start()
    for dz in range(1, A):
        out.relay(dz)
    share_mg.start(0)
    gains.finish()
    gain_rows = jnp.sum(GP[...], axis=0)
    r["GN"][...] = gain_rows

    def norm_one_step(i):
        rows = aligned(i * step_rows, step_rows)
        N1[rows, :] = (RT[rows, :].astype(f32) * R1[rows, :] * r["GN"][0:1]).astype(bf16)

    loop(4, norm_one_step)
    qkv.relay_own()
    for dz in range(1, A):
        qkv.relay_second(dz)
    out.relay_own()
    for dz in range(1, A):
        qkv.relay_third(dz)
    qkv.finish()

    def project(i):
        cols = aligned((i % 4) * quart, quart)
        g = i // 4
        QKVM[g, :, cols] = dot(N1[...], WA[g, :, :, cols].reshape(D, quart), 1, 0).astype(bf16)

    loop(12, project)
    for dz in range(1, A):
        out.relay_second(dz)
    for dz in range(1, A):
        out.relay_third(dz)
    for dz in range(1, A):
        up.relay(dz)
    down.start()

    lane = lax.broadcasted_iota(jnp.int32, (1, LANES), 1)
    low_lanes = lane < HEAD_DIM
    causal = lax.broadcasted_iota(jnp.int32, (CAP, CAP), 0) >= lax.broadcasted_iota(jnp.int32, (CAP, CAP), 1)

    def pick(h, v):
        return jnp.where(low_lanes if h == 0 else ~low_lanes, v, jnp.zeros_like(v))

    def place(i):
        return aligned((i // (D // LANES)) * CAP, CAP), aligned((i % (D // LANES)) * LANES, LANES)

    def softmax_of(s, q, k, h):
        logits = dot(pick(h, q), k, 1, 1) * scale
        same = SEGC[s][:, 0:1] == SEGR[s][0:1]
        logits = jnp.where(causal & same, logits, -1e30)
        e = jnp.exp(logits - jnp.max(logits, axis=-1, keepdims=True))
        return e * (1.0 / jnp.sum(e, axis=-1, keepdims=True))

    def attend(i):
        rows, cols = place(i)
        s = i // (D // LANES)
        q, k, v = QKVM[0, rows, cols], QKVM[1, rows, cols], QKVM[2, rows, cols]
        o = [dot(softmax_of(s, q, k, h).astype(bf16), v, 1, 0) for h in range(2)]
        QKVM[3, rows, cols] = jnp.where(low_lanes, o[0], o[1]).astype(bf16)

    pairs = S * (D // LANES)
    loop(pairs, attend)
    out.finish()

    def project_out(i):
        cols = aligned(i * quart, quart)
        AO[:, cols] = dot(QKVM[3], WA[3, :, :, cols].reshape(D, quart), 1, 0)

    loop(4, project_out)

    def norm_two(k):
        def step(i):
            rows = aligned(k * rows_half + i * (rows_half // 2), rows_half // 2)
            v = RT[rows, :].astype(f32) + AO[rows, :]
            scale_two = lax.rsqrt(jnp.mean(v * v, axis=-1, keepdims=True) + EPS)
            R2[rows, :] = scale_two
            part = (v * scale_two * r["GN"][1:2]).astype(bf16)
            NT[n, pl.ds(k * (A // 2) + i * (A // 4), A // 4)] = part.reshape(A // 4, 2, RB, D)

        loop(2, step)

    for k in range(2):
        norm_two(k)
        share_nt.start(k)
    share_mg.start(1)

    def block_of(ref, b):
        return ref.at[b // 2, pl.ds((b % 2) * (A // 2), A // 2)]

    tanh_k = math.sqrt(2.0 / math.pi)

    def up_block(b):
        rows = NT[b].reshape(T, D)

        def step(i):
            cols = aligned(i * quart, quart)
            v = dot(NT[b].reshape(T, D), WU[:, :, :, cols].reshape(D, quart), 1, 0)
            vv = v * v
            t = jnp.tanh(tanh_k * v * (1.0 + 0.044715 * vv))
            act = 0.5 * v * (1.0 + t)
            slope = 0.5 * (1.0 + t) + 0.5 * v * (1.0 - t * t) * (tanh_k * (1.0 + 0.134145 * vv))
            block_of(ACT, b)[..., cols] = act.astype(bf16).reshape(A // 2, 2, 2, RB, quart)
            block_of(DG, b)[..., cols] = slope.astype(bf16).reshape(A // 2, 2, 2, RB, quart)

        loop(4, step)

    up.finish()
    up_block(n)
    for k in range(2):
        share_nt.core[k].wait_recv()
    up_block(y * 2 + 1 - c)
    for dz in range(1, A):
        down.relay(dz)
    for k in range(2):
        share_mg.relay(k) if k == 0 else None
        share_nt.relay(k)
    share_mg.relay(1)
    up_block((1 - y) * 2 + c)
    for k in range(2):
        share_nt.last[k].wait_recv()
    up_block((1 - y) * 2 + 1 - c)
    for k in range(2):
        share_mg.core[k].wait_recv()
        share_mg.last[k].wait_recv()
    down.finish()

    def act_grad_step(i):
        b, j = i // 4, i % 4
        cols = aligned(j * quart, quart)
        rows = WD[pl.ds(j * (A // 4), A // 4)].reshape(quart, D)
        v = dot(MG[b], rows, 1, 1)
        at = block_of(DG, b)
        slope = at[..., cols].reshape(T, quart).astype(f32)
        at[..., cols] = (v * slope).astype(bf16).reshape(A // 2, 2, 2, RB, quart)

    loop(16, act_grad_step)

    class NarrowReduce:
        def __init__(self, part, k, total):
            self.part, self.k, self.total = part, k, total

        def run(self, b, store):
            def step(j):
                cols = aligned(j * quart, quart)
                store(cols, self.part(b, j))

            loop(4, step)

        def start(self):
            self.core = []
            for q, yy in enumerate((1 - y, y)):

                def put(cols, v, q=q):
                    PS[q, :, cols] = v.astype(bf16)

                self.run(yy * 2 + 1 - c, put)
                self.core.append(links.go(PS.at[q], PR.at[q], to_c))
            self.core[0].wait_recv()

            def put_far(cols, v):
                YS[:, cols] = (v + PR[0, :, cols].astype(f32)).astype(bf16)

            self.run((1 - y) * 2 + c, put_far)
            self.far = links.go(YS, YR.at[self.k], to_y)
            self.core[1].wait_recv()

            def put_own(cols, v):
                self.total[:, cols] = v + PR[1, :, cols].astype(f32)

            self.run(n, put_own)

    def norm_two_part(b, j):
        rows = WU[pl.ds(j * (A // 4), A // 4)].reshape(quart, D)
        return dot(block_of(DG, b)[...].reshape(T, D), rows, 1, 1)

    def mlp_part(b, j):
        cols = aligned(j * quart, quart)
        return dot(block_of(ACT, b)[...].reshape(T, D), WD[:, :, :, cols].reshape(D, quart), 1, 0)

    reduce_nt = NarrowReduce(norm_two_part, 0, NG)
    reduce_nt.start()
    pl.semaphore_signal(credit.at[0], inc=1, device_id=to_c, device_id_type=MESH)

    class WideReduce:
        def __init__(self, grad, k):
            self.grad, self.k = grad, k

        def compute(self, lhs, rhs):
            def step(i):
                cols = aligned(i * quart, quart)
                v = dot(lhs(cols), rhs(), 0, 0)
                self.grad[pl.ds(i * (A // 4), A // 4)] = v.astype(bf16).reshape(A // 4, 2, R, D)

            loop(4, step)

        def start(self):
            self.x = {}
            for dz in list(range(1, A)) + [0]:
                self.x[dz] = links.go(self.grad.at[ahead[dz], 1 - x], r["GXR"].at[self.k, dz], to_x)

        def middle(self):
            self.far = {}
            for dz in list(range(1, A)) + [0]:
                self.x[dz].wait_recv()
                p = self.grad.at[ahead[dz], x]
                p[...] = (p[...].astype(f32) + r["GXR"][self.k, dz].astype(f32)).astype(bf16)
                if dz:
                    self.far[dz] = links.go(p, r["GZR"].at[self.k, dz - 1], dev(ahead[dz], x, y, c))

        def last(self):
            total = self.grad[z, x].astype(f32)
            for dz in range(1, A):
                self.far[dz].wait_recv()
                total = total + r["GZR"][self.k, dz - 1].astype(f32)
            r["FIN"][self.k, n] = total.astype(bf16)
            p = r["FIN"].at[self.k, n]
            self.core = [links.go(p, p, to_c)]
            self.yy = links.go(p, p, to_y)

        def finish(self):
            self.yy.wait_recv()
            p = r["FIN"].at[self.k, (1 - y) * 2 + c]
            self.core.append(links.go(p, p, to_c))
            for copy in self.core:
                copy.wait_recv()

    reduce_up, reduce_down = WideReduce(WU, 0), WideReduce(WD, 1)
    up.release()
    reduce_up.compute(lambda cols: NT[..., cols].reshape(4 * T, quart), lambda: DG[...].reshape(4 * T, D))
    reduce_up.start()
    share_nt.release()
    pl.semaphore_signal(credit.at[1], inc=1, device_id=to_c, device_id_type=MESH)

    reduce_mo = NarrowReduce(mlp_part, 1, MO)
    pl.semaphore_wait(credit.at[0], 1)
    links.sent_all(reduce_nt.core)
    links.sent(reduce_nt.far)
    reduce_mo.start()
    down.release()
    reduce_down.compute(lambda cols: ACT[..., cols].reshape(4 * T, quart), lambda: MG[...].reshape(4 * T, D))
    reduce_down.start()
    reduce_up.middle()

    reduce_nt.far.wait_recv()
    links.sent_all(reduce_mo.core)
    SM[...] = jnp.zeros_like(SM)

    def norm_two_back(i):
        rows = aligned(i * step_rows, step_rows)
        dy = NG[rows, :] + YR[0, rows, :].astype(f32)
        v = RT[rows, :].astype(f32) + AO[rows, :]
        s2 = R2[rows, :]
        dyg = dy * r["GN"][1:2]
        mean = jnp.mean(dyg * v, axis=-1, keepdims=True)
        grad = s2 * dyg - v * (s2 * s2 * s2 * mean)
        SM[1:2] += jnp.sum(dy * (v * s2), axis=0, keepdims=True)
        NG[rows, :] = grad
        PS[0, rows, :] = (GATE[rows, :] * OG[rows, :].astype(f32) + grad).astype(bf16)

    loop(4, norm_two_back)

    class AttnReduce:
        def __init__(self, buf, at, k):
            self.buf, self.at, self.k = buf, at, k

        def compute(self, lhs, rhs):
            def step(i):
                cols = aligned(i * quart, quart)
                v = dot(lhs(cols), rhs(), 0, 0)
                self.buf[self.at, pl.ds(i * (A // 4), A // 4)] = v.astype(bf16).reshape(A // 4, 2, 2, RB, D)

            loop(4, step)

        def start(self):
            self.core = [links.go(self.buf.at[self.at, :, :, 1 - c], NT.at[self.k], to_c)]

        def part(self, zz, xx, cols=None):
            if cols is None:
                return self.buf.at[self.at, zz, xx, c]
            return self.buf.at[self.at, zz, xx, c, :, aligned(cols * half, half)]

        def first(self):
            self.core[0].wait_recv()

            def step(i):
                p = self.buf.at[self.at, i // 2, i % 2, c]
                p[...] = (p[...].astype(f32) + NT[self.k, i // 2, i % 2].astype(f32)).astype(bf16)

            loop(2 * A, step)
            self.one, self.two, self.far = {}, {}, {}
            for dz in range(A):
                d = (dz + 1) % A
                zz = ahead[d]
                if d < A // 2:
                    self.one[d] = links.go(self.part(zz, 1 - x), r["XRA"].at[self.k, d], to_x)
                else:
                    e = d - A // 2
                    cols = aligned((1 - y) * half, half)
                    self.one[d] = links.go(self.buf.at[self.at, zz, :, c, :, cols], r["YRB"].at[self.k, e], to_y)

        def add(self, p, q):
            p[...] = (p[...].astype(f32) + q[...].astype(f32)).astype(bf16)

        def second(self):
            for dz in range(A):
                d = (dz + 1) % A
                zz = ahead[d]
                self.one[d].wait_recv()
                if d < A // 2:
                    self.add(self.part(zz, x), r["XRA"].at[self.k, d])
                    self.two[d] = links.go(self.part(zz, x, 1 - y), r["YRA"].at[self.k, d], to_y)
                else:
                    e = d - A // 2
                    p = self.buf.at[self.at, zz, :, c, :, aligned(y * half, half)]
                    self.add(p, r["YRB"].at[self.k, e])
                    self.two[d] = links.go(self.part(zz, 1 - x, y), r["XRB"].at[self.k, e], to_x)

        def third(self):
            for dz in range(A):
                d = (dz + 1) % A
                zz = ahead[d]
                self.two[d].wait_recv()
                p = self.part(zz, x, y)
                self.add(p, r["YRA"].at[self.k, d] if d < A // 2 else r["XRB"].at[self.k, d - A // 2])
                if d:
                    self.far[d] = links.go(p, r["ZR"].at[self.k, d - 1], dev(zz, x, y, c))

        def fin(self, yy):
            return r["FINA"].at[self.k, c, :, aligned(yy * half, half)]

        def last(self):
            total = self.part(z, x, y)[...].astype(f32)
            for d in range(1, A):
                self.far[d].wait_recv()
                total = total + r["ZR"][self.k, d - 1].astype(f32)
            p = self.fin(y)
            p[...] = total.astype(bf16)
            self.core.append(links.go(p, p, to_c))
            self.yy = links.go(p, p, to_y)

        def finish(self):
            self.yy.wait_recv()
            p = self.fin(1 - y)
            self.core.append(links.go(p, p, to_c))
            for copy in self.core[1:]:
                copy.wait_recv()

    reduce_o = AttnReduce(ACT, 0, 3)
    reduce_v = AttnReduce(ACT, 1, 2)
    reduce_k = AttnReduce(DG, 0, 1)
    reduce_q = AttnReduce(DG, 1, 0)
    reduce_o.compute(lambda cols: QKVM[3, :, cols], lambda: PS[0])
    pl.semaphore_wait(credit.at[1], 1)
    reduce_o.start()

    def mixed_back(j):
        rows = WA[3, pl.ds(j * (Wd // 4), Wd // 4)].reshape(quart, D)
        MG[3, :, aligned(j * quart, quart)] = dot(PS[0], rows, 1, 1).astype(bf16)

    share_mg.release()
    loop(4, mixed_back)
    reduce_o.first()
    reduce_down.middle()

    def attend_back(i):
        rows, cols = place(i)
        s = i // (D // LANES)
        q, k, v = QKVM[0, rows, cols], QKVM[1, rows, cols], QKVM[2, rows, cols]
        dm = MG[3, rows, cols]
        dq, dk, dv = [], [], []
        for h in range(2):
            p = softmax_of(s, q, k, h)
            dp = dot(pick(h, dm), v, 1, 1)
            dl = (p * (dp - jnp.sum(p * dp, axis=-1, keepdims=True))).astype(bf16)
            dq.append(dot(dl, k, 1, 0))
            dk.append(dot(dl, q, 0, 0))
            dv.append(dot(p.astype(bf16), dm, 0, 0))
        MG[0, rows, cols] = (jnp.where(low_lanes, dq[0], dq[1]) * scale).astype(bf16)
        MG[1, rows, cols] = (jnp.where(low_lanes, dk[0], dk[1]) * scale).astype(bf16)
        MG[2, rows, cols] = jnp.where(low_lanes, dv[0], dv[1]).astype(bf16)

    loop(pairs, attend_back)
    reduce_up.last()
    reduce_o.second()
    for k, red in ((2, reduce_v), (1, reduce_k), (0, reduce_q)):
        red.compute(lambda cols: N1[:, cols], lambda k=k: MG[k])
        red.start()
    reduce_v.first()
    reduce_k.first()
    reduce_q.first()
    reduce_o.third()
    reduce_up.finish()
    reduce_down.last()

    reduce_mo.far.wait_recv()

    def output_step(i):
        rows = aligned(i * step_rows, step_rows)
        v = RT[rows, :].astype(f32)
        g = OG[rows, :].astype(f32)
        gate = GATE[rows, :]
        branch = AO[rows, :] + MO[rows, :] + YR[1, rows, :].astype(f32)
        lg = jnp.sum(g * branch, axis=-1, keepdims=True) * gate * (1.0 - gate)
        LG[rows, :] = lg
        SM[2:3] += jnp.sum(lg * v, axis=0, keepdims=True)
        QKVM[3, rows, :] = (v + gate * branch).astype(bf16)

    loop(4, output_step)
    new_copy = pltpu.make_async_copy(QKVM.at[3], r["new_rows"], local.at[0])
    new_copy.start()

    reduce_v.second()
    reduce_k.second()
    reduce_q.second()
    reduce_v.third()
    reduce_down.finish()
    reduce_o.last()

    def norm_one_grad(j):
        rows = pl.ds(j * (Wd // 4), Wd // 4)
        v = dot(MG[0], WA[0, rows].reshape(quart, D), 1, 1)
        v = v + dot(MG[1], WA[1, rows].reshape(quart, D), 1, 1)
        v = v + dot(MG[2], WA[2, rows].reshape(quart, D), 1, 1)
        MO[:, aligned(j * quart, quart)] = v

    loop(4, norm_one_grad)

    def norm_one_back(i):
        rows = aligned(i * step_rows, step_rows)
        dy = MO[rows, :]
        v = RT[rows, :].astype(f32)
        s1 = R1[rows, :]
        dyg = dy * r["GN"][0:1]
        mean = jnp.mean(dyg * v, axis=-1, keepdims=True)
        SM[0:1] += jnp.sum(dy * (v * s1), axis=0, keepdims=True)
        grad = s1 * dyg - v * (s1 * s1 * s1 * mean)
        grad = OG[rows, :].astype(f32) + NG[rows, :] + grad + LG[rows, :] * router_row
        QKVM[0, rows, :] = grad.astype(bf16)

    loop(4, norm_one_back)
    grad_copy = pltpu.make_async_copy(QKVM.at[0], r["row_grads"], local.at[1])
    grad_copy.start()

    total = lambda v: jnp.sum(jnp.sum(v, axis=1, keepdims=True), axis=0, keepdims=True)
    chosen = total(jnp.sum(SEGR[...], axis=0)[1:2])
    lanes = lax.broadcasted_iota(jnp.int32, (1, D), 1)
    SM[3:4] = (
        jnp.where(lanes == 0, chosen, 0.0)
        + jnp.where(lanes == 1, total(STAT[1:2]), 0.0)
        + jnp.where(lanes == 2, total(STAT[0:1]), 0.0)
    )
    SMS, SMR, SMZ = r["SMS"], r["SMR"], r["SMZ"]
    sums = [links.go(SM, SMR.at[0], to_c)]
    reduce_k.third()
    sums[0].wait_recv()
    SMS[0] = SM[...] + SMR[0]
    sums.append(links.go(SMS.at[0], SMR.at[1], to_x))
    reduce_q.third()
    reduce_o.finish()
    sums[1].wait_recv()
    SMS[1] = SMS[0] + SMR[1]
    sums.append(links.go(SMS.at[1], SMR.at[2], to_y))
    reduce_v.last()
    sums[2].wait_recv()
    SMZ[z] = SMS[1] + SMR[2]
    sums = [links.go(SMZ.at[z], SMZ.at[z], dev(ahead[dz], x, y, c)) for dz in range(1, A)]
    reduce_k.last()
    reduce_q.last()
    for copy in sums:
        copy.wait_recv()
    r["small"][...] = jnp.sum(SMZ[...], axis=0)
    reduce_v.finish()
    reduce_k.finish()
    reduce_q.finish()
    outs = [
        pltpu.make_async_copy(r["FIN"], r["mlp_grads"], local.at[2]),
        pltpu.make_async_copy(r["FINA"], r["attn_grads"], local.at[3]),
    ]
    for copy in outs:
        copy.start()
    links.drain()
    for copy in outs + [new_copy, grad_copy]:
        copy.wait()
    for k, name in enumerate(DEBUG):
        copy = pltpu.make_async_copy(r[name], r["dbg_" + name], local.at[4])
        copy.start()
        copy.wait()


def scatter_kernel(rows_ref, slots_ref, base_ref, out_ref):
    k = pl.program_id(2)
    size = base_ref.shape[-2]
    cap = slots_ref.shape[-1]
    position = lax.broadcasted_iota(jnp.int32, (size, cap), 0) + k * size
    onehot = jnp.where(slots_ref[0] == position, 1.0, 0.0)
    hit = jnp.max(onehot, axis=-1, keepdims=True) > 0.5
    picked = dot(onehot.astype(bf16), rows_ref[0, 0], 1, 0)
    base = base_ref[0]
    out_ref[0] = jnp.where(hit, picked, base.astype(f32)).astype(bf16)


def scatter_rows(rows, slots, base):
    count, length, width = base.shape
    cap = slots.shape[1]
    size = 512
    return pl.pallas_call(
        scatter_kernel,
        grid=(1, count, length // size),
        out_shape=jax.ShapeDtypeStruct(base.shape, base.dtype),
        in_specs=[
            pl.BlockSpec((1, 1, cap, width), lambda a, s, k: (0, s, 0, 0)),
            pl.BlockSpec((1, 1, cap), lambda a, s, k: (s, 0, 0)),
            pl.BlockSpec((1, size, width), lambda a, s, k: (s, k, 0)),
        ],
        out_specs=pl.BlockSpec((1, size, width), lambda a, s, k: (s, k, 0)),
        compiler_params=pltpu.CompilerParams(vmem_limit_bytes=32 * MIB),
        name="scatter_rows",
    )(rows.reshape(1, count, cap, width), slots.reshape(count, 1, cap), base)


def run_block(mesh, inputs, S, SEQ, CAP, D, R):
    Wd = mesh.shape["wide"]
    A, RB, T = Wd // 2, R // 2, S * CAP
    dims = dict(A=A, R=R, T=T, S=S, CAP=CAP, SEQ=SEQ, D=D, RB=RB)
    out_shapes = {
        "new_rows": ((T, D), bf16),
        "row_grads": ((T, D), bf16),
        "mlp_grads": ((2, 4, R, D), bf16),
        "attn_grads": ((4, 2, RB, D), bf16),
        "small": ((8, D), f32),
    }
    scratch = {
        "WA": ((4, Wd, R, D), bf16),
        "WU": ((A, 2, R, D), bf16),
        "WD": ((A, 2, R, D), bf16),
        "GP": ((Wd, 8, D), f32),
        "GN": ((8, D), f32),
        "NT": ((4, A, 2, RB, D), bf16),
        "MG": ((4, T, D), bf16),
        "ACT": ((2, A, 2, 2, RB, D), bf16),
        "DG": ((2, A, 2, 2, RB, D), bf16),
        "QKVM": ((4, T, D), bf16),
        "N1": ((T, D), bf16),
        "RT": ((T, D), bf16),
        "OG": ((T, D), bf16),
        "AO": ((T, D), f32),
        "NG": ((T, D), f32),
        "MO": ((T, D), f32),
        "PS": ((2, T, D), bf16),
        "PR": ((2, T, D), bf16),
        "YS": ((T, D), bf16),
        "YR": ((2, T, D), bf16),
        "GXR": ((2, A, R, D), bf16),
        "GZR": ((2, A - 1, R, D), bf16),
        "FIN": ((2, 4, R, D), bf16),
        "XRA": ((4, A // 2, RB, D), bf16),
        "YRA": ((4, A // 2, RB, D // 2), bf16),
        "YRB": ((4, A // 2, 2, RB, D // 2), bf16),
        "XRB": ((4, A // 2, RB, D // 2), bf16),
        "ZR": ((4, A - 1, RB, D // 2), bf16),
        "FINA": ((4, 2, RB, D), bf16),
        "GATE": ((T, 1), f32),
        "R1": ((T, 1), f32),
        "R2": ((T, 1), f32),
        "LG": ((T, 1), f32),
        "SEGC": ((S, CAP, LANES), f32),
        "SEGR": ((S, 16, CAP), f32),
        "STAT": ((8, CHUNK), f32),
        "SM": ((8, D), f32),
        "SMS": ((2, 8, D), f32),
        "SMR": ((3, 8, D), f32),
        "SMZ": ((A, 8, D), f32),
    }
    for name in DEBUG:
        out_shapes["dbg_" + name] = scratch[name]
    count = copy_count(A)
    semaphores = {
        "send": pltpu.SemaphoreType.DMA((count,)),
        "recv": pltpu.SemaphoreType.DMA((count,)),
        "local": pltpu.SemaphoreType.DMA((11,)),
        "credit": pltpu.SemaphoreType.REGULAR((2,)),
    }
    in_vmem = ("gains", "router", "slots", "marks")
    hbm, vmem = pl.BlockSpec(memory_space=pl.ANY), pl.BlockSpec(memory_space=pltpu.VMEM)
    names = list(inputs) + list(out_shapes) + list(scratch) + list(semaphores)
    results = pl.pallas_call(
        functools.partial(block_kernel, dims, names),
        out_shape=[jax.ShapeDtypeStruct(*v) for v in out_shapes.values()],
        in_specs=[vmem if k in in_vmem else hbm for k in inputs],
        out_specs=[vmem if k == "small" else hbm for k in out_shapes],
        scratch_shapes=[pltpu.VMEM(*v) for v in scratch.values()] + list(semaphores.values()),
        compiler_params=pltpu.CompilerParams(
            collective_id=0, has_side_effects=True, vmem_limit_bytes=64 * MIB - 65536
        ),
        name="routed_block",
    )(*inputs.values())
    return dict(zip(out_shapes, results))


def body(mesh, block_input, query_weight, key_weight, value_weight, out_weight, up_weight, down_weight,
         attn_gain, mlp_gain, router_weight, slots, segments, pad_mask, cotangent):
    S, SEQ, D = block_input.shape
    CAP = slots.shape[1]
    R, FF = up_weight.shape
    Wd = mesh.shape["wide"]
    w, n = lax.axis_index("wide"), lax.axis_index("narrow")
    part = FF // (4 * Wd)
    assert FF == 4 * D and 2 * S * CAP == D and part == R and mesh.shape["narrow"] == 4
    w_up = lax.dynamic_index_in_dim(up_weight.reshape(R, Wd, 4, part), n, axis=2, keepdims=False)
    shard = jnp.stack([attn_gain, mlp_gain]).astype(f32)
    gains = lax.dynamic_update_slice(jnp.zeros((8, D), f32), shard, (0, w * R))
    marks = jnp.zeros((S, 16, SEQ), bf16)
    marks = marks.at[:, 0].set(segments.astype(bf16)).at[:, 1].set(pad_mask.astype(bf16))
    inputs = {
        "block_input": block_input,
        "cotangent": cotangent,
        "w_query": query_weight,
        "w_key": key_weight,
        "w_value": value_weight,
        "w_out": out_weight,
        "w_up": w_up.reshape(R, D),
        "w_down": down_weight,
        "gains": gains,
        "router": jnp.zeros((16, D), bf16).at[0].set(router_weight),
        "slots": slots.reshape(S, CAP, 1),
        "marks": marks,
    }
    res = run_block(mesh, inputs, S, SEQ, CAP, D, R)
    block_output = scatter_rows(res["new_rows"], slots, block_input)
    input_grad = scatter_rows(res["row_grads"], slots, cotangent)
    small = res["small"]
    attn = res["attn_grads"].reshape(4, R, D).astype(f32)
    mlp = res["mlp_grads"].astype(f32)
    grad_up = mlp[0].reshape(4, R, Wd, part).transpose(1, 2, 0, 3).reshape(R, FF)
    grad_down = mlp[1].reshape(4 * R, D)
    gain_grads = lax.dynamic_slice(small, (0, w * R), (2, R))
    statistics = jnp.stack([small[3, 0] / small[3, 1], small[3, 2] / small[3, 1]])
    result = (block_output, input_grad, attn[0], attn[1], attn[2], attn[3], grad_up, grad_down,
              gain_grads[0], gain_grads[1], small[2], statistics)
    if DEBUG:
        return result, {k: res["dbg_" + k] for k in DEBUG}
    return result


def solution(mesh):
    rows, wide = P(("wide", "narrow")), P("wide")
    return jax.shard_map(
        functools.partial(body, mesh),
        mesh=mesh,
        in_specs=(rows,) + (wide,) * 8 + (P(),) + (rows,) * 4,
        out_specs=(rows, rows) + (wide,) * 8 + (P(), P()),
        check_vma=False,
    )
```

time: 1740 us -> 339 us (0.19)
  waiting for transfers between devices: 1200 us -> 0 us
  Pallas kernels: 0 us -> 304 us
  local copies, waits for them, and re-layouts: 242 us -> 28.5 us
  matrix products: 146 us -> 0 us
  blocking collectives: 106 us -> 0 us
    reduce_scatter x6 -> x0, waiting for transfers between devices: 871 us -> none  [the longest x1 286 us: body(): lax.psum_scatter(grad_up, 'wide', scatter_dimension=0, tiled=True)]
    all_gather x6 -> x0, waiting for transfers between devices: 327 us -> none  [the longest x1 120 us: body(): lax.all_gather(down_weight, 'wide', axis=0, tiled=True)]
    pallas_call x0 -> x3, Pallas kernels: none -> 304 us  [the longest x1 291 us: run_block(): pl.pallas_call(functools.partial(block_kernel, dims, names), out_shape=[j...]
    scatter x2 -> x3, local copies, waits for them, and re-layouts: 149 us -> 0.78 us  [the longest x1 0.62 us: body(): jnp.zeros((16, D), bf16).at[0].set(router_weight)]
    dot_general x27 -> x0, matrix products: 146 us -> none  [the longest x1 18.9 us: body(): pre_act = jnp.dot(normed_two, w_up, preferred_element_type=f32)]
    psum x2 -> x0, blocking collectives: 46.5 us -> none  [the longest x1 40.3 us: body(): router_total = lax.psum(router_local, ('wide', 'narrow'))]
    all_gather x2 -> x0, blocking collectives: 38.5 us -> none  [the longest x1 22.2 us: body(): lax.all_gather(attn_gain, 'wide', axis=0, tiled=True)]
    unnamed x101 -> x18, local copies, waits for them, and re-layouts: 36 us -> 9.26 us
  transfers between devices with their start and end apart: 13 -> 0, of which waited for: 11 -> 0; matrix products, arithmetic and copies ran while one was open for 18% -> 0% of each run, Pallas kernels for 0% -> 0%
where the time goes in v1:
time: 339 us; the launch traced here: 338 us
  Pallas kernels  304 us (90%)
  local copies, waits for them, and re-layouts  28.5 us (8%)
  between operations  3.42 us (1%)
    pallas_call x1, Pallas kernels, run_block(): pl.pallas_call(functools.partial(block_kernel, dims, names), out_shape=[j...  291 us
    pallas_call x2, Pallas kernels, scatter_rows(): pl.pallas_call(scatter_kernel, grid=(1, count, length // size), out_shape...  12.3 us
    unnamed x18, local copies, waits for them, and re-layouts  9.26 us

profile of v1, /device:TPU:0, one launch (start us, length us, event | category | flops | bytes accessed | tf_op | source)
XLA Modules:
  0.0 338.5 jit_solution(9362584056755363010)
XLA Ops:
  0.6 1.3 reshape.157.slots_ref
  1.9 0.7 reshape.152
  2.6 0.7 convert_bitcast_fusion.1
  3.3 0.7 convert_bitcast_fusion
  4.1 0.6 scatter.10.refs_9_
  4.7 0.7 convert_dynamic-update-slice_fusion.refs_8_
  5.4 0.6 copy-done.7
  6.0 0.1 scatter.14.refs_11_
  6.2 0.0 copy-start.6
  6.2 0.6 copy-done.6
  6.8 1.5 copy.31.refs_10_
  8.4 1.8 reshape.150
  10.2 1.5 dynamic-slice_reduce_fusion
  11.7 0.8 copy.37
  12.5 291.5 %routed_block.1 = (bf16[512,1024]{1,0:T(8,128)(2,1)}, bf16[512,1024]{1,0:T(8,128)(2,1)}, bf16[2,4,128,1024]{3,2,1,0:T(8,128)(2,1)}, bf16[4,2,64,1024]{3,2,1,0:T(8,128)(2,1)}, f32[8,1024]{1,0:T(8,128)}) custom-call(bf16[2,2048,1024]{2,1,0:T(8,128)(2,1)} %base_ref.2, bf16[2,2048,1024]{2,1,0:T(8,128)(2,1)} %base_ref.3, bf16[128,1024]{1,0:T(8,128)(2,1)} %refs_2_.1, ...), custom_call_target="tpu_custom_call" | custom-call | tf_op jit(solution)/shard_map/routed_block/pallas_call | solution.py:885
  303.9 0.7 constant_dynamic-slice_fusion
  304.6 0.5 slice_bitcast_fusion
  305.1 1.4 fusion.2
  309.2 1.4 slice.102
  310.5 0.6 pad_maximum_fusion
  311.1 2.7 fusion.1
  313.8 0.0 copy-done.5
  313.8 1.7 fusion
  315.5 0.5 copy.35
  316.0 0.1 bitcast_bitcast_fusion
  316.1 1.4 copy.32
  317.5 0.0 copy-start.4
  317.5 1.9 reshape.159
  319.4 3.4 copy-done
  322.8 6.2 %scatter_rows.3 = bf16[2,2048,1024]{2,1,0:T(8,128)(2,1)} custom-call(bf16[1,2,256,1024]{3,2,1,0:T(8,128)(2,1)S(1)} %bitcast.35, s32[2,1,256]{2,1,0:T(1,128)S(1)} %copy-done.4, bf16[2,2048,1024]{2,1,0:T(8,128)(2,1)S(1)} %copy-done), custom_call_target="tpu_custom_call" | custom-call | tf_op jit(solution)/shard_map/scatter_rows/pallas_call | solution.py:805
  328.9 3.4 copy-done.1
  332.3 6.2 %scatter_rows.2 = bf16[2,2048,1024]{2,1,0:T(8,128)(2,1)} custom-call(bf16[1,2,256,1024]{3,2,1,0:T(8,128)(2,1)S(1)} %bitcast.34, s32[2,1,256]{2,1,0:T(1,128)S(1)} %copy-done.4, bf16[2,2048,1024]{2,1,0:T(8,128)(2,1)S(1)} %copy-done.1), custom_call_target="tpu_custom_call" | custom-call | tf_op jit(solution)/shard_map/scatter_rows/pallas_call | solution.py:805
  (13 shorter events, 0.1 us)
Async XLA Ops:
  5.4 0.6 copy-start.7
  6.2 0.7 copy-start.6
  311.1 2.7 copy-start.5
  317.5 1.9 copy-start.3
  317.5 1.9 copy-start.4
  319.4 3.4 copy-start
  322.8 6.2 %copy-start.2 = (bf16[512,1024]{1,0:T(8,128)(2,1)S(1)}, bf16[512,1024]{1,0:T(8,128)(2,1)}, u32[]{:S(2)}) copy-start(bf16[512,1024]{1,0:T(8,128)(2,1)} %get-tuple-element.53) | copy-start | bytes 3145732
  328.9 3.4 copy-start.1

commit v2 on v1

--- a/solution.py
+++ b/solution.py
@@ -114,10 +114,18 @@
         pltpu.make_async_copy(r["w_key"], WA.at[1, w], local.at[1]),
         pltpu.make_async_copy(r["w_value"], WA.at[2, w], local.at[2]),
         pltpu.make_async_copy(r["w_out"], WA.at[3, w], local.at[3]),
-        pltpu.make_async_copy(r["w_up"], WU.at[z, x], local.at[4]),
         pltpu.make_async_copy(r["w_down"].at[aligned(n * R, R)], WD.at[z, x], local.at[5]),
         pltpu.make_async_copy(r["gains"], GP.at[w], local.at[6]),
     ]
+    if r["w_up"].shape[1] == D:
+        own.append(pltpu.make_async_copy(r["w_up"], WU.at[z, x], local.at[4]))
+    else:
+        own += [
+            pltpu.make_async_copy(
+                r["w_up"].at[:, aligned((v * 4 + n) * R, R)], WU.at[z, x, :, pl.ds(v * R, R)], local.at[11 + v]
+            )
+            for v in range(Wd)
+        ]
     for copy in own:
         copy.start()
     fetches = {}
@@ -225,6 +233,12 @@
     SEGC[...] = jnp.zeros_like(SEGC)
     SEGR[...] = jnp.zeros_like(SEGR)
     STAT[...] = jnp.zeros_like(STAT)
+    eye = lax.broadcasted_iota(jnp.int32, (CAP, CAP), 0) == lax.broadcasted_iota(jnp.int32, (CAP, CAP), 1)
+    for s in range(S):
+        row = r["slots"][s : s + 1, :].astype(f32)
+        r["SLOT"][s] = jnp.sum(jnp.where(eye, row, 0.0), axis=1, keepdims=True).astype(jnp.int32)
+    router_row = r["router"][...].astype(f32)
+    router_tile = jnp.broadcast_to(router_row, (16, D)).astype(bf16)
     steps = S * (SEQ // CHUNK)
 
     def gather_step(i):
@@ -239,23 +253,24 @@
         for copy in fetch(i, slot):
             copy.wait()
         position = lax.broadcasted_iota(jnp.int32, (CAP, CHUNK), 1) + k * CHUNK
-        onehot = jnp.where(r["slots"][s] == position, 1.0, 0.0).astype(bf16)
+        onehot = jnp.where(r["SLOT"][s] == position, 1.0, 0.0).astype(bf16)
         rows = aligned(s * CAP, CAP)
         tokens = QKVM[2 * slot]
         AO[rows, :] += dot(onehot, tokens, 1, 0)
         NG[rows, :] += dot(onehot, QKVM[2 * slot + 1], 1, 0)
-        marks = r["marks"][s, :, aligned(k * CHUNK, CHUNK)]
-        mask = marks[1:2].astype(f32)
-        gate_logits = dot(r["router"][...], tokens, 1, 1)[0:1]
+        at = (pl.ds(s, 1), aligned(k * CHUNK, CHUNK))
+        segment, mask = r["segments"][at].astype(f32), r["pad_mask"][at].astype(f32)
+        line = lax.broadcasted_iota(jnp.int32, (16, CHUNK), 0)
+        marks = jnp.where(line == 0, segment, jnp.where(line == 1, mask, 0.0)).astype(bf16)
+        gate_logits = dot(router_tile, tokens, 1, 1)[0:1]
         STAT[0:1] += mask * jax.nn.sigmoid(gate_logits)
         STAT[1:2] += mask
         SEGR[s] += dot(marks, onehot, 1, 1)
-        SEGC[s] += dot(onehot, jnp.broadcast_to(marks[0:1].astype(f32), (LANES, CHUNK)).astype(bf16), 1, 1)
+        SEGC[s] += dot(onehot, jnp.broadcast_to(segment, (LANES, CHUNK)).astype(bf16), 1, 1)
 
     loop(steps, gather_step)
 
     step_rows = T // 4
-    router_row = r["router"][0:1].astype(f32)
 
     def gate_step(i):
         rows = aligned(i * step_rows, step_rows)
@@ -786,35 +801,99 @@
         copy.wait()
 
 
-def scatter_kernel(rows_ref, slots_ref, base_ref, out_ref):
-    k = pl.program_id(2)
-    size = base_ref.shape[-2]
-    cap = slots_ref.shape[-1]
+def finish_kernel(dims, slots, rows, row_grads, attn_grads, mlp_grads, small, base, base_grad,
+                  out, out_grad, stats, router, gain_one, gain_two, attn_out, up_out, down_out,
+                  attn_stage, up_stage, down_stage, sems):
+    S, per, R, Wd, part = dims
+    i = pl.program_id(0)
+    s, k = i // per, i % per
+    size, cap = base.shape[1], slots.shape[1]
     position = lax.broadcasted_iota(jnp.int32, (size, cap), 0) + k * size
-    onehot = jnp.where(slots_ref[0] == position, 1.0, 0.0)
+    onehot = jnp.where(slots[pl.ds(s, 1), :] == position, 1.0, 0.0)
     hit = jnp.max(onehot, axis=-1, keepdims=True) > 0.5
-    picked = dot(onehot.astype(bf16), rows_ref[0, 0], 1, 0)
-    base = base_ref[0]
-    out_ref[0] = jnp.where(hit, picked, base.astype(f32)).astype(bf16)
-
-
-def scatter_rows(rows, slots, base):
-    count, length, width = base.shape
-    cap = slots.shape[1]
-    size = 512
+    onehot = onehot.astype(bf16)
+    own = aligned(s * cap, cap)
+    for new, old, target in ((rows, base, out), (row_grads, base_grad, out_grad)):
+        picked = dot(onehot, new[own, :], 1, 0).astype(bf16)
+        target[0] = jnp.where(hit, picked, old[0])
+
+    attn_copies = [
+        pltpu.make_async_copy(attn_stage.at[g], attn_out[g], sems.at[g]) for g in range(4)
+    ]
+    down_copies = [
+        pltpu.make_async_copy(down_stage.at[q], down_out.at[pl.ds(q * R, R)], sems.at[4 + q]) for q in range(4)
+    ]
+    up_copy = pltpu.make_async_copy(up_stage, up_out, sems.at[8])
+
+    @pl.when(i == 0)
+    def _():
+        for g in range(4):
+            attn_stage[g] = attn_grads[g].astype(f32)
+            attn_copies[g].start()
+        w = lax.axis_index("wide")
+        gains = pltpu.roll(small[...], (small.shape[1] - w * R) % small.shape[1], 1)
+        gain_one[...] = gains[0:1, :R]
+        gain_two[...] = gains[1:2, :R]
+        router[...] = small[2:3]
+        lane = lax.broadcasted_iota(jnp.int32, (1, small.shape[1]), 1)
+        counts = small[3:4]
+        valid = jnp.sum(jnp.where(lane == 1, counts, 0.0), axis=1, keepdims=True)
+        shifted = jnp.where(lane == 1, pltpu.roll(counts, small.shape[1] - 1, 1), counts)
+        stats[...] = (shifted / valid)[:, : stats.shape[1]]
+
+    @pl.when(i == 1)
+    def _():
+        for q in range(4):
+            down_stage[q] = mlp_grads[1, q].astype(f32)
+            down_copies[q].start()
+
+    @pl.when(i == 2)
+    def _():
+        for q in range(4):
+            for v in range(Wd):
+                at = (v * 4 + q) * part
+                up_stage[:, at : at + part] = mlp_grads[0, q, :, v * part : (v + 1) * part].astype(f32)
+        up_copy.start()
+
+    @pl.when(i == S * per - 1)
+    def _():
+        for copy in attn_copies + down_copies + [up_copy]:
+            copy.wait()
+
+
+def finish(mesh, res, slots, block_input, cotangent, R, FF):
+    S, SEQ, D = block_input.shape
+    Wd = mesh.shape["wide"]
+    size = 256
+    per, part = SEQ // size, FF // (4 * Wd)
+
+    def kernel(slots, rows, row_grads, attn, mlp, small, base, base_grad, out, out_grad, stats, router,
+               gain_one, gain_two, q, k, v, o, up, down, *scratch):
+        finish_kernel((S, per, R, Wd, part), slots, rows, row_grads, attn, mlp, small, base, base_grad,
+                      out, out_grad, stats, router, gain_one, gain_two, (q, k, v, o), up, down, *scratch)
+
+    vmem, hbm = pl.BlockSpec(memory_space=pltpu.VMEM), pl.BlockSpec(memory_space=pl.ANY)
+    tile = pl.BlockSpec((1, size, D), lambda i: (i // per, i % per, 0))
+    shape = jax.ShapeDtypeStruct
     return pl.pallas_call(
-        scatter_kernel,
-        grid=(1, count, length // size),
-        out_shape=jax.ShapeDtypeStruct(base.shape, base.dtype),
-        in_specs=[
-            pl.BlockSpec((1, 1, cap, width), lambda a, s, k: (0, s, 0, 0)),
-            pl.BlockSpec((1, 1, cap), lambda a, s, k: (s, 0, 0)),
-            pl.BlockSpec((1, size, width), lambda a, s, k: (s, k, 0)),
+        kernel,
+        grid=(S * per,),
+        out_shape=[shape(block_input.shape, bf16)] * 2
+        + [shape((1, 2), f32), shape((1, D), f32), shape((1, R), f32), shape((1, R), f32)]
+        + [shape((R, D), f32)] * 4
+        + [shape((R, FF), f32), shape((4 * R, D), f32)],
+        in_specs=[vmem] * 6 + [tile] * 2,
+        out_specs=[tile] * 2 + [vmem] * 4 + [hbm] * 6,
+        scratch_shapes=[
+            pltpu.VMEM((4, R, D), f32),
+            pltpu.VMEM((R, FF), f32),
+            pltpu.VMEM((4, R, D), f32),
+            pltpu.SemaphoreType.DMA((9,)),
         ],
-        out_specs=pl.BlockSpec((1, size, width), lambda a, s, k: (s, k, 0)),
-        compiler_params=pltpu.CompilerParams(vmem_limit_bytes=32 * MIB),
-        name="scatter_rows",
-    )(rows.reshape(1, count, cap, width), slots.reshape(count, 1, cap), base)
+        compiler_params=pltpu.CompilerParams(vmem_limit_bytes=60 * MIB),
+        name="finish_rows",
+    )(slots, res["new_rows"], res["row_grads"], res["attn_grads"].reshape(4, R, D), res["mlp_grads"],
+      res["small"], block_input, cotangent)
 
 
 def run_block(mesh, inputs, S, SEQ, CAP, D, R):
@@ -862,6 +941,7 @@
         "R1": ((T, 1), f32),
         "R2": ((T, 1), f32),
         "LG": ((T, 1), f32),
+        "SLOT": ((S, CAP, 1), jnp.int32),
         "SEGC": ((S, CAP, LANES), f32),
         "SEGR": ((S, 16, CAP), f32),
         "STAT": ((8, CHUNK), f32),
@@ -876,10 +956,10 @@
     semaphores = {
         "send": pltpu.SemaphoreType.DMA((count,)),
         "recv": pltpu.SemaphoreType.DMA((count,)),
-        "local": pltpu.SemaphoreType.DMA((11,)),
+        "local": pltpu.SemaphoreType.DMA((11 + Wd,)),
         "credit": pltpu.SemaphoreType.REGULAR((2,)),
     }
-    in_vmem = ("gains", "router", "slots", "marks")
+    in_vmem = ("gains", "router", "slots", "segments", "pad_mask")
     hbm, vmem = pl.BlockSpec(memory_space=pl.ANY), pl.BlockSpec(memory_space=pltpu.VMEM)
     names = list(inputs) + list(out_shapes) + list(scratch) + list(semaphores)
     results = pl.pallas_call(
@@ -905,11 +985,11 @@
     w, n = lax.axis_index("wide"), lax.axis_index("narrow")
     part = FF // (4 * Wd)
     assert FF == 4 * D and 2 * S * CAP == D and part == R and mesh.shape["narrow"] == 4
-    w_up = lax.dynamic_index_in_dim(up_weight.reshape(R, Wd, 4, part), n, axis=2, keepdims=False)
+    if part % LANES:
+        up_weight = lax.dynamic_index_in_dim(up_weight.reshape(R, Wd, 4, part), n, axis=2, keepdims=False)
+        up_weight = up_weight.reshape(R, D)
     shard = jnp.stack([attn_gain, mlp_gain]).astype(f32)
     gains = lax.dynamic_update_slice(jnp.zeros((8, D), f32), shard, (0, w * R))
-    marks = jnp.zeros((S, 16, SEQ), bf16)
-    marks = marks.at[:, 0].set(segments.astype(bf16)).at[:, 1].set(pad_mask.astype(bf16))
     inputs = {
         "block_input": block_input,
         "cotangent": cotangent,
@@ -917,25 +997,17 @@
         "w_key": key_weight,
         "w_value": value_weight,
         "w_out": out_weight,
-        "w_up": w_up.reshape(R, D),
+        "w_up": up_weight,
         "w_down": down_weight,
         "gains": gains,
-        "router": jnp.zeros((16, D), bf16).at[0].set(router_weight),
-        "slots": slots.reshape(S, CAP, 1),
-        "marks": marks,
+        "router": router_weight.reshape(1, D),
+        "slots": slots,
+        "segments": segments,
+        "pad_mask": pad_mask,
     }
     res = run_block(mesh, inputs, S, SEQ, CAP, D, R)
-    block_output = scatter_rows(res["new_rows"], slots, block_input)
-    input_grad = scatter_rows(res["row_grads"], slots, cotangent)
-    small = res["small"]
-    attn = res["attn_grads"].reshape(4, R, D).astype(f32)
-    mlp = res["mlp_grads"].astype(f32)
-    grad_up = mlp[0].reshape(4, R, Wd, part).transpose(1, 2, 0, 3).reshape(R, FF)
-    grad_down = mlp[1].reshape(4 * R, D)
-    gain_grads = lax.dynamic_slice(small, (0, w * R), (2, R))
-    statistics = jnp.stack([small[3, 0] / small[3, 1], small[3, 2] / small[3, 1]])
-    result = (block_output, input_grad, attn[0], attn[1], attn[2], attn[3], grad_up, grad_down,
-              gain_grads[0], gain_grads[1], small[2], statistics)
+    outs = finish(mesh, res, slots, block_input, cotangent, R, FF)
+    result = (outs[0], outs[1], *outs[6:], outs[4].reshape(R), outs[5].reshape(R), outs[3].reshape(D), outs[2].reshape(2))
     if DEBUG:
         return result, {k: res["dbg_" + k] for k in DEBUG}
     return result

time: 339 us -> 318 us (0.938)
  local copies, waits for them, and re-layouts: 28.5 us -> 1.9 us
  Pallas kernels: 304 us -> 313 us
    unnamed x18 -> x0, local copies, waits for them, and re-layouts: 9.26 us -> none
    pallas_call x2 -> x1, Pallas kernels: 12.3 us -> 21.6 us  [finish(): pl.pallas_call(kernel, grid=(S * per,), out_shape=[shape(block_input.shap...]
    slice x4 -> x0, local copies, waits for them, and re-layouts: 7.13 us -> none  [the longest x1 2.72 us: body(): attn[3]]
    reshape x4 -> x1, local copies, waits for them, and re-layouts: 6.44 us -> 1.28 us  [body(): router_weight.reshape(1, D)]
where the time goes in v2:
time: 318 us; the launch traced here: 317 us
  Pallas kernels  313 us (98%)
    pallas_call x1, Pallas kernels, run_block(): pl.pallas_call(functools.partial(block_kernel, dims, names), out_shape=[j...  291 us
    pallas_call x1, Pallas kernels, finish(): pl.pallas_call(kernel, grid=(S * per,), out_shape=[shape(block_input.shap...  21.6 us

profile of v2, /device:TPU:0, one launch (start us, length us, event | category | flops | bytes accessed | tf_op | source)
XLA Modules:
  0.0 316.8 jit_solution(7212842887438784430)
XLA Ops:
  0.6 1.3 reshape.42.refs_9_
  1.9 0.6 broadcast_in_dim.3
  2.5 1.2 convert_dynamic-update-slice_fusion.refs_8_
  3.8 291.3 %routed_block.1 = (bf16[512,1024]{1,0:T(8,128)(2,1)}, bf16[512,1024]{1,0:T(8,128)(2,1)}, bf16[2,4,128,1024]{3,2,1,0:T(8,128)(2,1)}, bf16[4,2,64,1024]{3,2,1,0:T(8,128)(2,1)}, f32[8,1024]{1,0:T(8,128)}) custom-call(bf16[2,2048,1024]{2,1,0:T(8,128)(2,1)} %base.1, bf16[2,2048,1024]{2,1,0:T(8,128)(2,1)} %base_grad.1, bf16[128,1024]{1,0:T(8,128)(2,1)} %refs_2_.1, ...), custom_call_target="tpu_custom_call" | custom-call | tf_op jit(solution)/shard_map/routed_block/pallas_call | solution.py:965
  295.1 21.6 %finish_rows.1 = (bf16[2,2048,1024]{2,1,0:T(8,128)(2,1)}, bf16[2,2048,1024]{2,1,0:T(8,128)(2,1)}, f32[1,2]{1,0:T(1,128)}, f32[1,1024]{1,0:T(1,128)}, f32[1,128]{...) custom-call(s32[2,256]{1,0:T(2,128)} %slots.1, ...), custom_call_target="tpu_custom_call" | custom-call | tf_op jit(solution)/shard_map/finish_rows/pallas_call | solution.py:878

commit v3 on v2

--- a/solution.py
+++ b/solution.py
@@ -34,6 +34,17 @@
         return carry
 
     lax.fori_loop(0, count, run, 0)
+
+
+class Column:
+    def __init__(self, ref, lane):
+        self.ref, self.lane = ref, slice(lane, lane + 1)
+
+    def __getitem__(self, at):
+        return self.ref[at[0], self.lane]
+
+    def __setitem__(self, at, value):
+        self.ref[at[0], self.lane] = value
 
 
 class Links:
@@ -74,8 +85,8 @@
 
 def copy_count(far):
     near = far - 1
-    gather = 2 * (8 * near + 2) + 3 * (2 * near + 1)
-    narrow = 2 * 6 + 2 * 3
+    gather = 4 * (8 * near + 2) + 3 * (2 * near + 1)
+    narrow = 2 * 6 + 2 * 4
     reduce_mlp = 2 * (far + near + 3)
     reduce_attn = 4 * (1 + 2 * far + near + 3)
     return gather + narrow + reduce_mlp + reduce_attn + 3 + near
@@ -97,8 +108,8 @@
     QKVM, N1, RT, OG = r["QKVM"], r["N1"], r["RT"], r["OG"]
     AO, NG, MO = r["AO"], r["NG"], r["MO"]
     PS, PR, YS, YR = r["PS"], r["PR"], r["YS"], r["YR"]
-    GATE, R1, R2, LG = r["GATE"], r["R1"], r["R2"], r["LG"]
-    SEGC, SEGR, STAT, SM = r["SEGC"], r["SEGR"], r["STAT"], r["SM"]
+    GATE, R1, R2, LG, SLOT = (Column(r["COLS"], k) for k in range(5))
+    SEGR, STAT, SM = r["SEGR"], r["STAT"], r["SM"]
     local, credit = r["local"], r["credit"]
     links = Links(r["send"], r["recv"])
 
@@ -206,7 +217,11 @@
         def start(self):
             p = self.at(z, x)
             self.far = {dz: links.go(p, p, dev(ahead[dz], x, y, c)) for dz in range(1, A)}
-            self.near = [links.go(p, p, to_x)]
+            self.near = []
+
+        def start_near(self):
+            p = self.at(z, x)
+            self.near.append(links.go(p, p, to_x))
 
         def relay(self, dz):
             self.far[dz].wait_recv()
@@ -221,22 +236,28 @@
             links.sent_all(list(self.far.values()) + self.near)
 
     gains = WideGather(lambda zz, xx: GP.at[zz * 2 + xx])
-    qkv, out = AttnGather(0, 3), AttnGather(3, 1)
+    query, key, value, out = (AttnGather(g, 1) for g in range(4))
+    attn = (query, key, value, out)
     up = WideGather(lambda zz, xx: WU.at[zz, xx])
     down = WideGather(lambda zz, xx: WD.at[zz, xx])
     gains.start()
-    qkv.start()
-    out.start()
+    gains.start_near()
+    for group in attn:
+        group.start()
+    up.start()
+    down.start()
 
     AO[...] = jnp.zeros_like(AO)
     NG[...] = jnp.zeros_like(NG)
-    SEGC[...] = jnp.zeros_like(SEGC)
     SEGR[...] = jnp.zeros_like(SEGR)
     STAT[...] = jnp.zeros_like(STAT)
     eye = lax.broadcasted_iota(jnp.int32, (CAP, CAP), 0) == lax.broadcasted_iota(jnp.int32, (CAP, CAP), 1)
+
+    def upright(row):
+        return jnp.sum(jnp.where(eye, row, 0.0), axis=1, keepdims=True)
+
     for s in range(S):
-        row = r["slots"][s : s + 1, :].astype(f32)
-        r["SLOT"][s] = jnp.sum(jnp.where(eye, row, 0.0), axis=1, keepdims=True).astype(jnp.int32)
+        SLOT[pl.ds(s * CAP, CAP), :] = upright(r["slots"][s : s + 1, :].astype(f32))
     router_row = r["router"][...].astype(f32)
     router_tile = jnp.broadcast_to(router_row, (16, D)).astype(bf16)
     steps = S * (SEQ // CHUNK)
@@ -253,8 +274,8 @@
         for copy in fetch(i, slot):
             copy.wait()
         position = lax.broadcasted_iota(jnp.int32, (CAP, CHUNK), 1) + k * CHUNK
-        onehot = jnp.where(r["SLOT"][s] == position, 1.0, 0.0).astype(bf16)
         rows = aligned(s * CAP, CAP)
+        onehot = jnp.where(SLOT[rows, :].astype(jnp.int32) == position, 1.0, 0.0).astype(bf16)
         tokens = QKVM[2 * slot]
         AO[rows, :] += dot(onehot, tokens, 1, 0)
         NG[rows, :] += dot(onehot, QKVM[2 * slot + 1], 1, 0)
@@ -266,9 +287,31 @@
         STAT[0:1] += mask * jax.nn.sigmoid(gate_logits)
         STAT[1:2] += mask
         SEGR[s] += dot(marks, onehot, 1, 1)
-        SEGC[s] += dot(onehot, jnp.broadcast_to(segment, (LANES, CHUNK)).astype(bf16), 1, 1)
-
-    loop(steps, gather_step)
+
+    def gather_steps(first, last):
+        loop(last - first, lambda i: gather_step(i + first))
+
+    far = range(1, A)
+    gather_steps(0, 3)
+    for dz in far:
+        gains.relay(dz)
+    for dz in far:
+        query.relay(dz)
+    gather_steps(3, 5)
+    for dz in far:
+        key.relay(dz)
+    query.relay_own()
+    for dz in far:
+        query.relay_second(dz)
+    gather_steps(5, 7)
+    for dz in far:
+        value.relay(dz)
+    key.relay_own()
+    for dz in far:
+        key.relay_second(dz)
+    for dz in far:
+        query.relay_third(dz)
+    gather_steps(7, steps)
 
     step_rows = T // 4
 
@@ -282,6 +325,13 @@
         OG[rows, :] = g.astype(bf16)
         MG[n, rows, :] = (gate * g).astype(bf16)
 
+    for dz in far:
+        out.relay(dz)
+    value.relay_own()
+    for dz in far:
+        value.relay_second(dz)
+    for dz in far:
+        key.relay_third(dz)
     loop(4, gate_step)
 
     class RowShare:
@@ -305,86 +355,78 @@
             for copies in (self.core, self.far, self.last):
                 links.sent_all(list(copies.values()))
 
-    rows_half = T // 2
-    share_mg = RowShare(lambda b, k: MG.at[b, pl.ds(k * rows_half, rows_half)])
+    share_mg = RowShare(lambda b, k: MG.at[b, pl.ds(k * CAP, CAP)])
     share_nt = RowShare(lambda b, k: NT.at[b, pl.ds(k * (A // 2), A // 2)])
-
-    for dz in range(1, A):
-        gains.relay(dz)
-    for dz in range(1, A):
-        qkv.relay(dz)
-    up.start()
-    for dz in range(1, A):
-        out.relay(dz)
-    share_mg.start(0)
     gains.finish()
-    gain_rows = jnp.sum(GP[...], axis=0)
-    r["GN"][...] = gain_rows
+    r["GN"][...] = jnp.sum(GP[...], axis=0)
 
     def norm_one_step(i):
         rows = aligned(i * step_rows, step_rows)
         N1[rows, :] = (RT[rows, :].astype(f32) * R1[rows, :] * r["GN"][0:1]).astype(bf16)
 
     loop(4, norm_one_step)
-    qkv.relay_own()
-    for dz in range(1, A):
-        qkv.relay_second(dz)
+    ordered = lax.broadcasted_iota(jnp.int32, (CAP, CAP), 0) <= lax.broadcasted_iota(jnp.int32, (CAP, CAP), 1)
+    for s in range(S):
+        same = upright(SEGR[s][0:1]) == SEGR[s][0:1]
+        r["BIAS"][s] = jnp.where(ordered & same, 0.0, -1e30)
     out.relay_own()
-    for dz in range(1, A):
-        qkv.relay_third(dz)
-    qkv.finish()
-
-    def project(i):
-        cols = aligned((i % 4) * quart, quart)
-        g = i // 4
-        QKVM[g, :, cols] = dot(N1[...], WA[g, :, :, cols].reshape(D, quart), 1, 0).astype(bf16)
-
-    loop(12, project)
-    for dz in range(1, A):
+    for dz in far:
         out.relay_second(dz)
-    for dz in range(1, A):
+    for dz in far:
+        value.relay_third(dz)
+    for dz in far:
         out.relay_third(dz)
-    for dz in range(1, A):
-        up.relay(dz)
-    down.start()
+    up.start_near()
+    down.start_near()
+    for k in range(2):
+        share_mg.start(k)
+
+    def project(g):
+        def step(j):
+            cols = aligned(j * half, half)
+            QKVM[g, :, cols] = dot(N1[...], WA[g, :, :, cols].reshape(D, half), 1, 0).astype(bf16)
+
+        loop(2, step)
+
+    for g in range(3):
+        attn[g].finish()
+        project(g)
 
     lane = lax.broadcasted_iota(jnp.int32, (1, LANES), 1)
     low_lanes = lane < HEAD_DIM
-    causal = lax.broadcasted_iota(jnp.int32, (CAP, CAP), 0) >= lax.broadcasted_iota(jnp.int32, (CAP, CAP), 1)
 
     def pick(h, v):
         return jnp.where(low_lanes if h == 0 else ~low_lanes, v, jnp.zeros_like(v))
 
-    def place(i):
-        return aligned((i // (D // LANES)) * CAP, CAP), aligned((i % (D // LANES)) * LANES, LANES)
-
     def softmax_of(s, q, k, h):
-        logits = dot(pick(h, q), k, 1, 1) * scale
-        same = SEGC[s][:, 0:1] == SEGR[s][0:1]
-        logits = jnp.where(causal & same, logits, -1e30)
-        e = jnp.exp(logits - jnp.max(logits, axis=-1, keepdims=True))
-        return e * (1.0 / jnp.sum(e, axis=-1, keepdims=True))
-
-    def attend(i):
-        rows, cols = place(i)
-        s = i // (D // LANES)
-        q, k, v = QKVM[0, rows, cols], QKVM[1, rows, cols], QKVM[2, rows, cols]
-        o = [dot(softmax_of(s, q, k, h).astype(bf16), v, 1, 0) for h in range(2)]
-        QKVM[3, rows, cols] = jnp.where(low_lanes, o[0], o[1]).astype(bf16)
-
-    pairs = S * (D // LANES)
-    loop(pairs, attend)
-    out.finish()
-
-    def project_out(i):
-        cols = aligned(i * quart, quart)
-        AO[:, cols] = dot(QKVM[3], WA[3, :, :, cols].reshape(D, quart), 1, 0)
-
-    loop(4, project_out)
+        logits = dot(k, pick(h, q), 1, 1) + r["BIAS"][s]
+        e = jnp.exp(logits - jnp.max(logits, axis=0, keepdims=True))
+        return e * (1.0 / jnp.sum(e, axis=0, keepdims=True))
+
+    group = 2
+
+    def attend(s):
+        def step(i):
+            for u in range(group):
+                rows, cols = pl.ds(s * CAP, CAP), aligned((i * group + u) * LANES, LANES)
+                q, k, v = QKVM[0, rows, cols] * bf16(scale), QKVM[1, rows, cols], QKVM[2, rows, cols]
+                o = [dot(softmax_of(s, q, k, h).astype(bf16), v, 0, 0) for h in range(2)]
+                QKVM[3, rows, cols] = jnp.where(low_lanes, o[0], o[1]).astype(bf16)
+
+        loop(D // LANES // group, step)
+
+    def project_out(s):
+        rows = pl.ds(s * CAP, CAP)
+
+        def step(j):
+            cols = aligned(j * half, half)
+            AO[rows, cols] = dot(QKVM[3, rows, :], WA[3, :, :, cols].reshape(D, half), 1, 0)
+
+        loop(2, step)
 
     def norm_two(k):
         def step(i):
-            rows = aligned(k * rows_half + i * (rows_half // 2), rows_half // 2)
+            rows = aligned(k * CAP + i * (CAP // 2), CAP // 2)
             v = RT[rows, :].astype(f32) + AO[rows, :]
             scale_two = lax.rsqrt(jnp.mean(v * v, axis=-1, keepdims=True) + EPS)
             R2[rows, :] = scale_two
@@ -393,111 +435,121 @@
 
         loop(2, step)
 
+    attend(0)
+    out.finish()
+    project_out(0)
+    norm_two(0)
+    share_nt.start(0)
+    for dz in far:
+        up.relay(dz)
+    attend(1)
+    project_out(1)
+    norm_two(1)
+    share_nt.start(1)
+
+    tanh_k = math.sqrt(2.0 / math.pi)
+
+    def up_unit(yy, k):
+        rows = NT.at[pl.ds(yy * 2, 2), pl.ds(k * (A // 2), A // 2)]
+        parts = [pl.ds(cc * (A // 2) + k * (A // 4), A // 4) for cc in range(2)]
+
+        def step(j):
+            cols = aligned(j * quart, quart)
+            v = dot(rows[...].reshape(T, D), WU[:, :, :, cols].reshape(D, quart), 1, 0)
+            vv = v * v
+            t = jnp.tanh(v * (tanh_k + (tanh_k * 0.044715) * vv))
+            act = 0.5 * v * (1.0 + t)
+            slope = (0.5 + 0.5 * t) * (1.0 + v * (1.0 - t) * (tanh_k + (tanh_k * 0.134145) * vv))
+            for cc in range(2):
+                at = slice(cc * CAP, (cc + 1) * CAP)
+                ACT[yy, parts[cc], :, :, :, cols] = act[at].astype(bf16).reshape(A // 4, 2, 2, RB, quart)
+                DG[yy, parts[cc], :, :, :, cols] = slope[at].astype(bf16).reshape(A // 4, 2, 2, RB, quart)
+
+        loop(4, step)
+
+    def act_unit(yy):
+        def step(j):
+            cols = aligned(j * quart, quart)
+            rows = WD[pl.ds(j * (A // 4), A // 4)].reshape(quart, D)
+            v = dot(MG[pl.ds(yy * 2, 2)].reshape(2 * T, D), rows, 1, 1)
+            slope = DG[yy, :, :, :, :, cols].reshape(2 * T, quart).astype(f32)
+            DG[yy, :, :, :, :, cols] = (v * slope).astype(bf16).reshape(A, 2, 2, RB, quart)
+
+        loop(4, step)
+
+    up.finish()
+    share_nt.core[0].wait_recv()
+    up_unit(y, 0)
+    for dz in far:
+        down.relay(dz)
+    share_nt.core[1].wait_recv()
+    up_unit(y, 1)
     for k in range(2):
-        norm_two(k)
-        share_nt.start(k)
-    share_mg.start(1)
-
-    def block_of(ref, b):
-        return ref.at[b // 2, pl.ds((b % 2) * (A // 2), A // 2)]
-
-    tanh_k = math.sqrt(2.0 / math.pi)
-
-    def up_block(b):
-        rows = NT[b].reshape(T, D)
-
-        def step(i):
-            cols = aligned(i * quart, quart)
-            v = dot(NT[b].reshape(T, D), WU[:, :, :, cols].reshape(D, quart), 1, 0)
-            vv = v * v
-            t = jnp.tanh(tanh_k * v * (1.0 + 0.044715 * vv))
-            act = 0.5 * v * (1.0 + t)
-            slope = 0.5 * (1.0 + t) + 0.5 * v * (1.0 - t * t) * (tanh_k * (1.0 + 0.134145 * vv))
-            block_of(ACT, b)[..., cols] = act.astype(bf16).reshape(A // 2, 2, 2, RB, quart)
-            block_of(DG, b)[..., cols] = slope.astype(bf16).reshape(A // 2, 2, 2, RB, quart)
-
-        loop(4, step)
-
-    up.finish()
-    up_block(n)
-    for k in range(2):
-        share_nt.core[k].wait_recv()
-    up_block(y * 2 + 1 - c)
-    for dz in range(1, A):
-        down.relay(dz)
-    for k in range(2):
-        share_mg.relay(k) if k == 0 else None
-        share_nt.relay(k)
-    share_mg.relay(1)
-    up_block((1 - y) * 2 + c)
-    for k in range(2):
-        share_nt.last[k].wait_recv()
-    up_block((1 - y) * 2 + 1 - c)
+        share_mg.relay(k)
+    share_nt.relay(0)
+    down.finish()
     for k in range(2):
         share_mg.core[k].wait_recv()
+    act_unit(y)
+    share_nt.last[0].wait_recv()
+    up_unit(1 - y, 0)
+    share_nt.relay(1)
+    for k in range(2):
         share_mg.last[k].wait_recv()
-    down.finish()
-
-    def act_grad_step(i):
-        b, j = i // 4, i % 4
-        cols = aligned(j * quart, quart)
-        rows = WD[pl.ds(j * (A // 4), A // 4)].reshape(quart, D)
-        v = dot(MG[b], rows, 1, 1)
-        at = block_of(DG, b)
-        slope = at[..., cols].reshape(T, quart).astype(f32)
-        at[..., cols] = (v * slope).astype(bf16).reshape(A // 2, 2, 2, RB, quart)
-
-    loop(16, act_grad_step)
+    share_nt.last[1].wait_recv()
+    up_unit(1 - y, 1)
+    act_unit(1 - y)
 
     class NarrowReduce:
-        def __init__(self, part, k, total):
-            self.part, self.k, self.total = part, k, total
-
-        def run(self, b, store):
+        def __init__(self, lhs, part, send, k, total):
+            self.lhs, self.part, self.send, self.k, self.total = lhs, part, send, k, total
+            self.core, self.far = [], []
+
+        def compute(self, q):
+            yy = y if q else 1 - y
+            keep = self.total if q else MO
+
             def step(j):
                 cols = aligned(j * quart, quart)
-                store(cols, self.part(b, j))
+                v = self.part(self.lhs[yy].reshape(2 * T, D), j, cols)
+                PS[q, :, cols] = jnp.where(c == 0, v[T:], v[:T]).astype(bf16)
+                keep[:, cols] = jnp.where(c == 0, v[:T], v[T:])
 
             loop(4, step)
-
-        def start(self):
-            self.core = []
-            for q, yy in enumerate((1 - y, y)):
-
-                def put(cols, v, q=q):
-                    PS[q, :, cols] = v.astype(bf16)
-
-                self.run(yy * 2 + 1 - c, put)
-                self.core.append(links.go(PS.at[q], PR.at[q], to_c))
+            self.core.append(links.go(PS.at[q], PR.at[q], to_c))
+
+        def send_far(self):
             self.core[0].wait_recv()
-
-            def put_far(cols, v):
-                YS[:, cols] = (v + PR[0, :, cols].astype(f32)).astype(bf16)
-
-            self.run((1 - y) * 2 + c, put_far)
-            self.far = links.go(YS, YR.at[self.k], to_y)
+            for k in range(2):
+                rows = pl.ds(k * CAP, CAP)
+                self.send[rows, :] = (MO[rows, :] + PR[0, rows, :].astype(f32)).astype(bf16)
+                self.far.append(links.go(self.send.at[rows], YR.at[self.k, rows], to_y))
+
+        def keep_own(self):
             self.core[1].wait_recv()
-
-            def put_own(cols, v):
-                self.total[:, cols] = v + PR[1, :, cols].astype(f32)
-
-            self.run(n, put_own)
-
-    def norm_two_part(b, j):
-        rows = WU[pl.ds(j * (A // 4), A // 4)].reshape(quart, D)
-        return dot(block_of(DG, b)[...].reshape(T, D), rows, 1, 1)
-
-    def mlp_part(b, j):
-        cols = aligned(j * quart, quart)
-        return dot(block_of(ACT, b)[...].reshape(T, D), WD[:, :, :, cols].reshape(D, quart), 1, 0)
-
-    reduce_nt = NarrowReduce(norm_two_part, 0, NG)
-    reduce_nt.start()
+            for k in range(2):
+                rows = pl.ds(k * CAP, CAP)
+                self.total[rows, :] = self.total[rows, :] + PR[1, rows, :].astype(f32)
+
+    def norm_two_part(rows, j, cols):
+        return dot(rows, WU[pl.ds(j * (A // 4), A // 4)].reshape(quart, D), 1, 1)
+
+    def mlp_part(rows, j, cols):
+        return dot(rows, WD[:, :, :, cols].reshape(D, quart), 1, 0)
+
+    reduce_nt = NarrowReduce(DG, norm_two_part, YS, 0, NG)
+    reduce_nt.compute(0)
+    reduce_nt.compute(1)
+    reduce_nt.send_far()
+    reduce_nt.keep_own()
     pl.semaphore_signal(credit.at[0], inc=1, device_id=to_c, device_id_type=MESH)
 
     class WideReduce:
         def __init__(self, grad, k):
             self.grad, self.k = grad, k
+
+        def landing(self, dz):
+            return PR.at[0, pl.ds(dz * R, R)] if self.k else r["GXR"].at[dz]
 
         def compute(self, lhs, rhs):
             def step(i):
@@ -508,16 +560,15 @@
             loop(4, step)
 
         def start(self):
-            self.x = {}
+            self.x, self.far = {}, {}
             for dz in list(range(1, A)) + [0]:
-                self.x[dz] = links.go(self.grad.at[ahead[dz], 1 - x], r["GXR"].at[self.k, dz], to_x)
-
-        def middle(self):
-            self.far = {}
-            for dz in list(range(1, A)) + [0]:
+                self.x[dz] = links.go(self.grad.at[ahead[dz], 1 - x], self.landing(dz), to_x)
+
+        def middle(self, *dzs):
+            for dz in dzs:
                 self.x[dz].wait_recv()
                 p = self.grad.at[ahead[dz], x]
-                p[...] = (p[...].astype(f32) + r["GXR"][self.k, dz].astype(f32)).astype(bf16)
+                p[...] = (p[...].astype(f32) + self.landing(dz)[...].astype(f32)).astype(bf16)
                 if dz:
                     self.far[dz] = links.go(p, r["GZR"].at[self.k, dz - 1], dev(ahead[dz], x, y, c))
 
@@ -545,33 +596,67 @@
     share_nt.release()
     pl.semaphore_signal(credit.at[1], inc=1, device_id=to_c, device_id_type=MESH)
 
-    reduce_mo = NarrowReduce(mlp_part, 1, MO)
+    reduce_mo = NarrowReduce(ACT, mlp_part, r["YS2"], 1, MO)
     pl.semaphore_wait(credit.at[0], 1)
     links.sent_all(reduce_nt.core)
-    links.sent(reduce_nt.far)
-    reduce_mo.start()
+    reduce_mo.compute(0)
+    reduce_up.middle(1)
+    reduce_mo.send_far()
+    reduce_mo.compute(1)
+    reduce_mo.keep_own()
+    pl.semaphore_signal(credit.at[2], inc=1, device_id=to_x, device_id_type=MESH)
     down.release()
     reduce_down.compute(lambda cols: ACT[..., cols].reshape(4 * T, quart), lambda: MG[...].reshape(4 * T, D))
+    pl.semaphore_wait(credit.at[2], 1)
     reduce_down.start()
-    reduce_up.middle()
-
-    reduce_nt.far.wait_recv()
+    reduce_up.middle(2)
     links.sent_all(reduce_mo.core)
+    share_mg.release()
     SM[...] = jnp.zeros_like(SM)
 
-    def norm_two_back(i):
-        rows = aligned(i * step_rows, step_rows)
-        dy = NG[rows, :] + YR[0, rows, :].astype(f32)
-        v = RT[rows, :].astype(f32) + AO[rows, :]
-        s2 = R2[rows, :]
-        dyg = dy * r["GN"][1:2]
-        mean = jnp.mean(dyg * v, axis=-1, keepdims=True)
-        grad = s2 * dyg - v * (s2 * s2 * s2 * mean)
-        SM[1:2] += jnp.sum(dy * (v * s2), axis=0, keepdims=True)
-        NG[rows, :] = grad
-        PS[0, rows, :] = (GATE[rows, :] * OG[rows, :].astype(f32) + grad).astype(bf16)
-
-    loop(4, norm_two_back)
+    def norm_two_back(s):
+        def step(i):
+            rows = aligned(s * CAP + i * step_rows, step_rows)
+            dy = NG[rows, :] + YR[0, rows, :].astype(f32)
+            v = RT[rows, :].astype(f32) + AO[rows, :]
+            s2 = R2[rows, :]
+            dyg = dy * r["GN"][1:2]
+            mean = jnp.mean(dyg * v, axis=-1, keepdims=True)
+            grad = s2 * dyg - v * (s2 * s2 * s2 * mean)
+            SM[1:2] += jnp.sum(dy * (v * s2), axis=0, keepdims=True)
+            NG[rows, :] = grad
+            PS[0, rows, :] = (GATE[rows, :] * OG[rows, :].astype(f32) + grad).astype(bf16)
+
+        loop(2, step)
+
+    def mixed_back(s):
+        rows = pl.ds(s * CAP, CAP)
+
+        def step(j):
+            weight = WA[3, pl.ds(j * (Wd // 2), Wd // 2)].reshape(half, D)
+            MG[3, rows, aligned(j * half, half)] = dot(PS[0, rows, :], weight, 1, 1).astype(bf16)
+
+        loop(2, step)
+
+    def attend_back(s):
+        def step(i):
+            for u in range(group):
+                rows, cols = pl.ds(s * CAP, CAP), aligned((i * group + u) * LANES, LANES)
+                q, k, v = QKVM[0, rows, cols] * bf16(scale), QKVM[1, rows, cols], QKVM[2, rows, cols]
+                dm = MG[3, rows, cols]
+                dq, dk, dv = [], [], []
+                for h in range(2):
+                    p = softmax_of(s, q, k, h)
+                    dp = dot(v, pick(h, dm), 1, 1)
+                    dl = (p * (dp - jnp.sum(p * dp, axis=0, keepdims=True))).astype(bf16)
+                    dq.append(dot(dl, k, 0, 0))
+                    dk.append(dot(dl, q, 1, 0))
+                    dv.append(dot(p.astype(bf16), dm, 1, 0))
+                MG[0, rows, cols] = (jnp.where(low_lanes, dq[0], dq[1]) * scale).astype(bf16)
+                MG[1, rows, cols] = jnp.where(low_lanes, dk[0], dk[1]).astype(bf16)
+                MG[2, rows, cols] = jnp.where(low_lanes, dv[0], dv[1]).astype(bf16)
+
+        loop(D // LANES // group, step)
 
     class AttnReduce:
         def __init__(self, buf, at, k):
@@ -584,6 +669,9 @@
                 self.buf[self.at, pl.ds(i * (A // 4), A // 4)] = v.astype(bf16).reshape(A // 4, 2, 2, RB, D)
 
             loop(4, step)
+
+        def landing(self, d):
+            return PR.at[1, pl.ds((self.k * (A // 2) + d) * RB, RB)]
 
         def start(self):
             self.core = [links.go(self.buf.at[self.at, :, :, 1 - c], NT.at[self.k], to_c)]
@@ -606,7 +694,7 @@
                 d = (dz + 1) % A
                 zz = ahead[d]
                 if d < A // 2:
-                    self.one[d] = links.go(self.part(zz, 1 - x), r["XRA"].at[self.k, d], to_x)
+                    self.one[d] = links.go(self.part(zz, 1 - x), self.landing(d), to_x)
                 else:
                     e = d - A // 2
                     cols = aligned((1 - y) * half, half)
@@ -621,7 +709,7 @@
                 zz = ahead[d]
                 self.one[d].wait_recv()
                 if d < A // 2:
-                    self.add(self.part(zz, x), r["XRA"].at[self.k, d])
+                    self.add(self.part(zz, x), self.landing(d))
                     self.two[d] = links.go(self.part(zz, x, 1 - y), r["YRA"].at[self.k, d], to_y)
                 else:
                     e = d - A // 2
@@ -663,50 +751,28 @@
     reduce_v = AttnReduce(ACT, 1, 2)
     reduce_k = AttnReduce(DG, 0, 1)
     reduce_q = AttnReduce(DG, 1, 0)
+    reduce_nt.far[0].wait_recv()
+    norm_two_back(0)
+    mixed_back(0)
+    attend_back(0)
+    reduce_up.middle(3, 0) if A == 4 else reduce_up.middle(*range(3, A), 0)
+    reduce_nt.far[1].wait_recv()
+    norm_two_back(1)
+    mixed_back(1)
     reduce_o.compute(lambda cols: QKVM[3, :, cols], lambda: PS[0])
     pl.semaphore_wait(credit.at[1], 1)
     reduce_o.start()
-
-    def mixed_back(j):
-        rows = WA[3, pl.ds(j * (Wd // 4), Wd // 4)].reshape(quart, D)
-        MG[3, :, aligned(j * quart, quart)] = dot(PS[0], rows, 1, 1).astype(bf16)
-
-    share_mg.release()
-    loop(4, mixed_back)
+    attend_back(1)
     reduce_o.first()
-    reduce_down.middle()
-
-    def attend_back(i):
-        rows, cols = place(i)
-        s = i // (D // LANES)
-        q, k, v = QKVM[0, rows, cols], QKVM[1, rows, cols], QKVM[2, rows, cols]
-        dm = MG[3, rows, cols]
-        dq, dk, dv = [], [], []
-        for h in range(2):
-            p = softmax_of(s, q, k, h)
-            dp = dot(pick(h, dm), v, 1, 1)
-            dl = (p * (dp - jnp.sum(p * dp, axis=-1, keepdims=True))).astype(bf16)
-            dq.append(dot(dl, k, 1, 0))
-            dk.append(dot(dl, q, 0, 0))
-            dv.append(dot(p.astype(bf16), dm, 0, 0))
-        MG[0, rows, cols] = (jnp.where(low_lanes, dq[0], dq[1]) * scale).astype(bf16)
-        MG[1, rows, cols] = (jnp.where(low_lanes, dk[0], dk[1]) * scale).astype(bf16)
-        MG[2, rows, cols] = jnp.where(low_lanes, dv[0], dv[1]).astype(bf16)
-
-    loop(pairs, attend_back)
-    reduce_up.last()
-    reduce_o.second()
+    reduce_down.middle(1, 2)
     for k, red in ((2, reduce_v), (1, reduce_k), (0, reduce_q)):
         red.compute(lambda cols: N1[:, cols], lambda k=k: MG[k])
         red.start()
     reduce_v.first()
+    reduce_up.last()
     reduce_k.first()
+    reduce_down.middle(*range(3, A), 0)
     reduce_q.first()
-    reduce_o.third()
-    reduce_up.finish()
-    reduce_down.last()
-
-    reduce_mo.far.wait_recv()
 
     def output_step(i):
         rows = aligned(i * step_rows, step_rows)
@@ -719,16 +785,12 @@
         SM[2:3] += jnp.sum(lg * v, axis=0, keepdims=True)
         QKVM[3, rows, :] = (v + gate * branch).astype(bf16)
 
+    for copy in reduce_mo.far:
+        copy.wait_recv()
     loop(4, output_step)
     new_copy = pltpu.make_async_copy(QKVM.at[3], r["new_rows"], local.at[0])
     new_copy.start()
-
-    reduce_v.second()
-    reduce_k.second()
-    reduce_q.second()
-    reduce_v.third()
-    reduce_down.finish()
-    reduce_o.last()
+    reduce_o.second()
 
     def norm_one_grad(j):
         rows = pl.ds(j * (Wd // 4), Wd // 4)
@@ -738,6 +800,9 @@
         MO[:, aligned(j * quart, quart)] = v
 
     loop(4, norm_one_grad)
+    reduce_up.finish()
+    reduce_v.second()
+    reduce_o.third()
 
     def norm_one_back(i):
         rows = aligned(i * step_rows, step_rows)
@@ -765,25 +830,31 @@
     )
     SMS, SMR, SMZ = r["SMS"], r["SMR"], r["SMZ"]
     sums = [links.go(SM, SMR.at[0], to_c)]
-    reduce_k.third()
+    reduce_k.second()
+    reduce_v.third()
+    reduce_down.last()
     sums[0].wait_recv()
     SMS[0] = SM[...] + SMR[0]
     sums.append(links.go(SMS.at[0], SMR.at[1], to_x))
-    reduce_q.third()
-    reduce_o.finish()
+    reduce_q.second()
+    reduce_k.third()
+    reduce_o.last()
     sums[1].wait_recv()
     SMS[1] = SMS[0] + SMR[1]
     sums.append(links.go(SMS.at[1], SMR.at[2], to_y))
     reduce_v.last()
+    reduce_down.finish()
+    reduce_q.third()
     sums[2].wait_recv()
     SMZ[z] = SMS[1] + SMR[2]
     sums = [links.go(SMZ.at[z], SMZ.at[z], dev(ahead[dz], x, y, c)) for dz in range(1, A)]
     reduce_k.last()
+    reduce_o.finish()
+    reduce_v.finish()
     reduce_q.last()
     for copy in sums:
         copy.wait_recv()
     r["small"][...] = jnp.sum(SMZ[...], axis=0)
-    reduce_v.finish()
     reduce_k.finish()
     reduce_q.finish()
     outs = [
@@ -864,7 +935,7 @@
 def finish(mesh, res, slots, block_input, cotangent, R, FF):
     S, SEQ, D = block_input.shape
     Wd = mesh.shape["wide"]
-    size = 256
+    size = 512
     per, part = SEQ // size, FF // (4 * Wd)
 
     def kernel(slots, rows, row_grads, attn, mlp, small, base, base_grad, out, out_grad, stats, router,
@@ -927,22 +998,18 @@
         "PS": ((2, T, D), bf16),
         "PR": ((2, T, D), bf16),
         "YS": ((T, D), bf16),
+        "YS2": ((T, D), bf16),
         "YR": ((2, T, D), bf16),
-        "GXR": ((2, A, R, D), bf16),
+        "GXR": ((A, R, D), bf16),
         "GZR": ((2, A - 1, R, D), bf16),
         "FIN": ((2, 4, R, D), bf16),
-        "XRA": ((4, A // 2, RB, D), bf16),
         "YRA": ((4, A // 2, RB, D // 2), bf16),
         "YRB": ((4, A // 2, 2, RB, D // 2), bf16),
         "XRB": ((4, A // 2, RB, D // 2), bf16),
         "ZR": ((4, A - 1, RB, D // 2), bf16),
         "FINA": ((4, 2, RB, D), bf16),
-        "GATE": ((T, 1), f32),
-        "R1": ((T, 1), f32),
-        "R2": ((T, 1), f32),
-        "LG": ((T, 1), f32),
-        "SLOT": ((S, CAP, 1), jnp.int32),
-        "SEGC": ((S, CAP, LANES), f32),
+        "COLS": ((T, LANES), f32),
+        "BIAS": ((S, CAP, CAP), f32),
         "SEGR": ((S, 16, CAP), f32),
         "STAT": ((8, CHUNK), f32),
         "SM": ((8, D), f32),
@@ -957,7 +1024,7 @@
         "send": pltpu.SemaphoreType.DMA((count,)),
         "recv": pltpu.SemaphoreType.DMA((count,)),
         "local": pltpu.SemaphoreType.DMA((11 + Wd,)),
-        "credit": pltpu.SemaphoreType.REGULAR((2,)),
+        "credit": pltpu.SemaphoreType.REGULAR((3,)),
     }
     in_vmem = ("gains", "router", "slots", "segments", "pad_mask")
     hbm, vmem = pl.BlockSpec(memory_space=pl.ANY), pl.BlockSpec(memory_space=pltpu.VMEM)
@@ -984,7 +1051,7 @@
     Wd = mesh.shape["wide"]
     w, n = lax.axis_index("wide"), lax.axis_index("narrow")
     part = FF // (4 * Wd)
-    assert FF == 4 * D and 2 * S * CAP == D and part == R and mesh.shape["narrow"] == 4
+    assert FF == 4 * D and S == 2 and 4 * CAP == D and part == R and mesh.shape["narrow"] == 4
     if part % LANES:
         up_weight = lax.dynamic_index_in_dim(up_weight.reshape(R, Wd, 4, part), n, axis=2, keepdims=False)
         up_weight = up_weight.reshape(R, D)

time: 318 us -> 263 us (0.83)
  Pallas kernels: 313 us -> 257 us
    pallas_call x1, Pallas kernels: 291 us -> 239 us  [run_block(): pl.pallas_call(functools.partial(block_kernel, dims, names), out_shape=[j...]
    pallas_call x1, Pallas kernels: 21.6 us -> 18.2 us  [finish(): pl.pallas_call(kernel, grid=(S * per,), out_shape=[shape(block_input.shap...]
where the time goes in v3:
time: 263 us; the launch traced here: 261 us
  Pallas kernels  257 us (98%)
    pallas_call x1, Pallas kernels, run_block(): pl.pallas_call(functools.partial(block_kernel, dims, names), out_shape=[j...  239 us
    pallas_call x1, Pallas kernels, finish(): pl.pallas_call(kernel, grid=(S * per,), out_shape=[shape(block_input.shap...  18.2 us

profile of v3, /device:TPU:0, one launch (start us, length us, event | category | flops | bytes accessed | tf_op | source)
XLA Modules:
  0.0 261.1 jit_solution(17201356891145075306)
XLA Ops:
  0.6 1.3 reshape.42.refs_9_
  1.9 0.6 broadcast_in_dim.3
  2.5 1.2 convert_dynamic-update-slice_fusion.refs_8_
  3.8 238.9 %routed_block.1 = (bf16[512,1024]{1,0:T(8,128)(2,1)}, bf16[512,1024]{1,0:T(8,128)(2,1)}, bf16[2,4,128,1024]{3,2,1,0:T(8,128)(2,1)}, bf16[4,2,64,1024]{3,2,1,0:T(8,128)(2,1)}, f32[8,1024]{1,0:T(8,128)}) custom-call(bf16[2,2048,1024]{2,1,0:T(8,128)(2,1)} %base.1, bf16[2,2048,1024]{2,1,0:T(8,128)(2,1)} %base_grad.1, bf16[128,1024]{1,0:T(8,128)(2,1)} %refs_2_.1, ...), custom_call_target="tpu_custom_call" | custom-call | tf_op jit(solution)/shard_map/routed_block/pallas_call | solution.py:1032
  242.7 18.2 %finish_rows.1 = (bf16[2,2048,1024]{2,1,0:T(8,128)(2,1)}, bf16[2,2048,1024]{2,1,0:T(8,128)(2,1)}, f32[1,2]{1,0:T(1,128)}, f32[1,1024]{1,0:T(1,128)}, f32[1,128]{...) custom-call(s32[2,256]{1,0:T(2,128)} %slots.1, ...), custom_call_target="tpu_custom_call" | custom-call | tf_op jit(solution)/shard_map/finish_rows/pallas_call | solution.py:949

commit v4 on v3

--- a/solution.py
+++ b/solution.py
@@ -258,7 +258,7 @@
 
     for s in range(S):
         SLOT[pl.ds(s * CAP, CAP), :] = upright(r["slots"][s : s + 1, :].astype(f32))
-    router_row = r["router"][...].astype(f32)
+    router_row = r["gains"][2:3]
     router_tile = jnp.broadcast_to(router_row, (16, D)).astype(bf16)
     steps = S * (SEQ // CHUNK)
 
@@ -403,7 +403,7 @@
         e = jnp.exp(logits - jnp.max(logits, axis=0, keepdims=True))
         return e * (1.0 / jnp.sum(e, axis=0, keepdims=True))
 
-    group = 2
+    group = 4
 
     def attend(s):
         def step(i):
@@ -446,6 +446,8 @@
     project_out(1)
     norm_two(1)
     share_nt.start(1)
+    for dz in range(1, A - 1):
+        down.relay(dz)
 
     tanh_k = math.sqrt(2.0 / math.pi)
 
@@ -477,28 +479,25 @@
 
         loop(4, step)
 
-    up.finish()
-    share_nt.core[0].wait_recv()
-    up_unit(y, 0)
-    for dz in far:
-        down.relay(dz)
-    share_nt.core[1].wait_recv()
-    up_unit(y, 1)
     for k in range(2):
         share_mg.relay(k)
+        share_nt.core[k].wait_recv()
+        share_mg.core[k].wait_recv()
+    up.finish()
+    up_unit(y, 0)
+    down.relay(A - 1)
+    up_unit(y, 1)
     share_nt.relay(0)
-    down.finish()
-    for k in range(2):
-        share_mg.core[k].wait_recv()
-    act_unit(y)
     share_nt.last[0].wait_recv()
     up_unit(1 - y, 0)
-    share_nt.relay(1)
     for k in range(2):
         share_mg.last[k].wait_recv()
+    share_nt.relay(1)
     share_nt.last[1].wait_recv()
     up_unit(1 - y, 1)
+    down.finish()
     act_unit(1 - y)
+    act_unit(y)
 
     class NarrowReduce:
         def __init__(self, lhs, part, send, k, total):
@@ -644,19 +643,22 @@
                 rows, cols = pl.ds(s * CAP, CAP), aligned((i * group + u) * LANES, LANES)
                 q, k, v = QKVM[0, rows, cols] * bf16(scale), QKVM[1, rows, cols], QKVM[2, rows, cols]
                 dm = MG[3, rows, cols]
+                k_t = k.T
                 dq, dk, dv = [], [], []
                 for h in range(2):
                     p = softmax_of(s, q, k, h)
                     dp = dot(v, pick(h, dm), 1, 1)
                     dl = (p * (dp - jnp.sum(p * dp, axis=0, keepdims=True))).astype(bf16)
-                    dq.append(dot(dl, k, 0, 0))
+                    dq.append(dot(k_t[h * HEAD_DIM : (h + 1) * HEAD_DIM], dl, 1, 0))
                     dk.append(dot(dl, q, 1, 0))
                     dv.append(dot(p.astype(bf16), dm, 1, 0))
-                MG[0, rows, cols] = (jnp.where(low_lanes, dq[0], dq[1]) * scale).astype(bf16)
+                MG[0, rows, cols] = (jnp.concatenate(dq, axis=0) * scale).astype(bf16).T
                 MG[1, rows, cols] = jnp.where(low_lanes, dk[0], dk[1]).astype(bf16)
                 MG[2, rows, cols] = jnp.where(low_lanes, dv[0], dv[1]).astype(bf16)
 
         loop(D // LANES // group, step)
+
+    x_first = A - A // 4
 
     class AttnReduce:
         def __init__(self, buf, at, k):
@@ -671,7 +673,9 @@
             loop(4, step)
 
         def landing(self, d):
-            return PR.at[1, pl.ds((self.k * (A // 2) + d) * RB, RB)]
+            if d < A // 2:
+                return PR.at[1, pl.ds((self.k * (A // 2) + d) * RB, RB)]
+            return r["XRA"].at[self.k, d - A // 2]
 
         def start(self):
             self.core = [links.go(self.buf.at[self.at, :, :, 1 - c], NT.at[self.k], to_c)]
@@ -693,10 +697,10 @@
             for dz in range(A):
                 d = (dz + 1) % A
                 zz = ahead[d]
-                if d < A // 2:
+                if d < x_first:
                     self.one[d] = links.go(self.part(zz, 1 - x), self.landing(d), to_x)
                 else:
-                    e = d - A // 2
+                    e = d - x_first
                     cols = aligned((1 - y) * half, half)
                     self.one[d] = links.go(self.buf.at[self.at, zz, :, c, :, cols], r["YRB"].at[self.k, e], to_y)
 
@@ -708,11 +712,11 @@
                 d = (dz + 1) % A
                 zz = ahead[d]
                 self.one[d].wait_recv()
-                if d < A // 2:
+                if d < x_first:
                     self.add(self.part(zz, x), self.landing(d))
                     self.two[d] = links.go(self.part(zz, x, 1 - y), r["YRA"].at[self.k, d], to_y)
                 else:
-                    e = d - A // 2
+                    e = d - x_first
                     p = self.buf.at[self.at, zz, :, c, :, aligned(y * half, half)]
                     self.add(p, r["YRB"].at[self.k, e])
                     self.two[d] = links.go(self.part(zz, 1 - x, y), r["XRB"].at[self.k, e], to_x)
@@ -723,7 +727,7 @@
                 zz = ahead[d]
                 self.two[d].wait_recv()
                 p = self.part(zz, x, y)
-                self.add(p, r["YRA"].at[self.k, d] if d < A // 2 else r["XRB"].at[self.k, d - A // 2])
+                self.add(p, r["YRA"].at[self.k, d] if d < x_first else r["XRB"].at[self.k, d - x_first])
                 if d:
                     self.far[d] = links.go(p, r["ZR"].at[self.k, d - 1], dev(zz, x, y, c))
 
@@ -935,7 +939,7 @@
 def finish(mesh, res, slots, block_input, cotangent, R, FF):
     S, SEQ, D = block_input.shape
     Wd = mesh.shape["wide"]
-    size = 512
+    size = 1024
     per, part = SEQ // size, FF // (4 * Wd)
 
     def kernel(slots, rows, row_grads, attn, mlp, small, base, base_grad, out, out_grad, stats, router,
@@ -1003,9 +1007,10 @@
         "GXR": ((A, R, D), bf16),
         "GZR": ((2, A - 1, R, D), bf16),
         "FIN": ((2, 4, R, D), bf16),
-        "YRA": ((4, A // 2, RB, D // 2), bf16),
-        "YRB": ((4, A // 2, 2, RB, D // 2), bf16),
-        "XRB": ((4, A // 2, RB, D // 2), bf16),
+        "XRA": ((4, A // 4, RB, D), bf16),
+        "YRA": ((4, A - A // 4, RB, D // 2), bf16),
+        "YRB": ((4, A // 4, 2, RB, D // 2), bf16),
+        "XRB": ((4, A // 4, RB, D // 2), bf16),
         "ZR": ((4, A - 1, RB, D // 2), bf16),
         "FINA": ((4, 2, RB, D), bf16),
         "COLS": ((T, LANES), f32),
@@ -1026,7 +1031,7 @@
         "local": pltpu.SemaphoreType.DMA((11 + Wd,)),
         "credit": pltpu.SemaphoreType.REGULAR((3,)),
     }
-    in_vmem = ("gains", "router", "slots", "segments", "pad_mask")
+    in_vmem = ("gains", "slots", "segments", "pad_mask")
     hbm, vmem = pl.BlockSpec(memory_space=pl.ANY), pl.BlockSpec(memory_space=pltpu.VMEM)
     names = list(inputs) + list(out_shapes) + list(scratch) + list(semaphores)
     results = pl.pallas_call(
@@ -1056,7 +1061,9 @@
         up_weight = lax.dynamic_index_in_dim(up_weight.reshape(R, Wd, 4, part), n, axis=2, keepdims=False)
         up_weight = up_weight.reshape(R, D)
     shard = jnp.stack([attn_gain, mlp_gain]).astype(f32)
-    gains = lax.dynamic_update_slice(jnp.zeros((8, D), f32), shard, (0, w * R))
+    line = lax.broadcasted_iota(jnp.int32, (8, D), 0)
+    gains = jnp.where(line == 2, router_weight.astype(f32)[None], 0.0)
+    gains = lax.dynamic_update_slice(gains, shard, (0, w * R))
     inputs = {
         "block_input": block_input,
         "cotangent": cotangent,
@@ -1067,7 +1074,6 @@
         "w_up": up_weight,
         "w_down": down_weight,
         "gains": gains,
-        "router": router_weight.reshape(1, D),
         "slots": slots,
         "segments": segments,
         "pad_mask": pad_mask,

time: 263 us -> 264 us (level)
    pallas_call x1, Pallas kernels: 239 us -> 242 us  [run_block(): pl.pallas_call(functools.partial(block_kernel, dims, names), out_shape=[j...]
where the time goes in v4:
time: 264 us; the launch traced here: 262 us
  Pallas kernels  258 us (98%)
    pallas_call x1, Pallas kernels, run_block(): pl.pallas_call(functools.partial(block_kernel, dims, names), out_shape=[j...  242 us
    pallas_call x1, Pallas kernels, finish(): pl.pallas_call(kernel, grid=(S * per,), out_shape=[shape(block_input.shap...  16.4 us

profile of v4, /device:TPU:0, one launch (start us, length us, event | category | flops | bytes accessed | tf_op | source)
XLA Modules:
  0.0 261.9 jit_solution(13062040467100534330)
XLA Ops:
  0.7 0.7 convert_element_type.6
  1.3 0.7 broadcast_select_fusion
  2.0 1.2 convert_dynamic-update-slice_fusion.refs_8_
  3.3 242.1 %routed_block.1 = (bf16[512,1024]{1,0:T(8,128)(2,1)}, bf16[512,1024]{1,0:T(8,128)(2,1)}, bf16[2,4,128,1024]{3,2,1,0:T(8,128)(2,1)}, bf16[4,2,64,1024]{3,2,1,0:T(8,128)(2,1)}, f32[8,1024]{1,0:T(8,128)}) custom-call(bf16[2,2048,1024]{2,1,0:T(8,128)(2,1)} %base.1, bf16[2,2048,1024]{2,1,0:T(8,128)(2,1)} %base_grad.1, bf16[128,1024]{1,0:T(8,128)(2,1)} %refs_2_.1, ...), custom_call_target="tpu_custom_call" | custom-call | tf_op jit(solution)/shard_map/routed_block/pallas_call | solution.py:1037
  245.3 16.4 %finish_rows.1 = (bf16[2,2048,1024]{2,1,0:T(8,128)(2,1)}, bf16[2,2048,1024]{2,1,0:T(8,128)(2,1)}, f32[1,2]{1,0:T(1,128)}, f32[1,1024]{1,0:T(1,128)}, f32[1,128]{...) custom-call(s32[2,256]{1,0:T(2,128)} %slots.1, ...), custom_call_target="tpu_custom_call" | custom-call | tf_op jit(solution)/shard_map/finish_rows/pallas_call | solution.py:953
  (1 shorter events, 0.0 us)

commit v5 on v4

--- a/solution.py
+++ b/solution.py
@@ -85,7 +85,7 @@
 
 def copy_count(far):
     near = far - 1
-    gather = 4 * (8 * near + 2) + 3 * (2 * near + 1)
+    gather = 4 * (8 * near + 2) + 5 * (2 * near + 1)
     narrow = 2 * 6 + 2 * 4
     reduce_mlp = 2 * (far + near + 3)
     reduce_attn = 4 * (1 + 2 * far + near + 3)
@@ -238,14 +238,16 @@
     gains = WideGather(lambda zz, xx: GP.at[zz * 2 + xx])
     query, key, value, out = (AttnGather(g, 1) for g in range(4))
     attn = (query, key, value, out)
-    up = WideGather(lambda zz, xx: WU.at[zz, xx])
-    down = WideGather(lambda zz, xx: WD.at[zz, xx])
+    up, down = (
+        [WideGather(lambda zz, xx, ref=ref, h=h: ref.at[zz, xx, pl.ds(h * RB, RB)]) for h in range(2)]
+        for ref in (WU, WD)
+    )
     gains.start()
     gains.start_near()
     for group in attn:
         group.start()
-    up.start()
-    down.start()
+    for part in up + down:
+        part.start()
 
     AO[...] = jnp.zeros_like(AO)
     NG[...] = jnp.zeros_like(NG)
@@ -376,8 +378,8 @@
         value.relay_third(dz)
     for dz in far:
         out.relay_third(dz)
-    up.start_near()
-    down.start_near()
+    for part in up + down:
+        part.start_near()
     for k in range(2):
         share_mg.start(k)
 
@@ -440,14 +442,15 @@
     project_out(0)
     norm_two(0)
     share_nt.start(0)
-    for dz in far:
-        up.relay(dz)
+    for part in up:
+        for dz in far:
+            part.relay(dz)
     attend(1)
     project_out(1)
     norm_two(1)
     share_nt.start(1)
-    for dz in range(1, A - 1):
-        down.relay(dz)
+    for dz in far:
+        down[0].relay(dz)
 
     tanh_k = math.sqrt(2.0 / math.pi)
 
@@ -483,9 +486,11 @@
         share_mg.relay(k)
         share_nt.core[k].wait_recv()
         share_mg.core[k].wait_recv()
-    up.finish()
+    for part in up:
+        part.finish()
     up_unit(y, 0)
-    down.relay(A - 1)
+    for dz in far:
+        down[1].relay(dz)
     up_unit(y, 1)
     share_nt.relay(0)
     share_nt.last[0].wait_recv()
@@ -495,7 +500,8 @@
     share_nt.relay(1)
     share_nt.last[1].wait_recv()
     up_unit(1 - y, 1)
-    down.finish()
+    for part in down:
+        part.finish()
     act_unit(1 - y)
     act_unit(y)
 
@@ -589,7 +595,8 @@
                 copy.wait_recv()
 
     reduce_up, reduce_down = WideReduce(WU, 0), WideReduce(WD, 1)
-    up.release()
+    for part in up:
+        part.release()
     reduce_up.compute(lambda cols: NT[..., cols].reshape(4 * T, quart), lambda: DG[...].reshape(4 * T, D))
     reduce_up.start()
     share_nt.release()
@@ -604,7 +611,8 @@
     reduce_mo.compute(1)
     reduce_mo.keep_own()
     pl.semaphore_signal(credit.at[2], inc=1, device_id=to_x, device_id_type=MESH)
-    down.release()
+    for part in down:
+        part.release()
     reduce_down.compute(lambda cols: ACT[..., cols].reshape(4 * T, quart), lambda: MG[...].reshape(4 * T, D))
     pl.semaphore_wait(credit.at[2], 1)
     reduce_down.start()
@@ -658,7 +666,7 @@
 
         loop(D // LANES // group, step)
 
-    x_first = A - A // 4
+    x_first = A // 2
 
     class AttnReduce:
         def __init__(self, buf, at, k):
@@ -673,9 +681,7 @@
             loop(4, step)
 
         def landing(self, d):
-            if d < A // 2:
-                return PR.at[1, pl.ds((self.k * (A // 2) + d) * RB, RB)]
-            return r["XRA"].at[self.k, d - A // 2]
+            return PR.at[1, pl.ds((self.k * (A // 2) + d) * RB, RB)]
 
         def start(self):
             self.core = [links.go(self.buf.at[self.at, :, :, 1 - c], NT.at[self.k], to_c)]
@@ -1007,10 +1013,9 @@
         "GXR": ((A, R, D), bf16),
         "GZR": ((2, A - 1, R, D), bf16),
         "FIN": ((2, 4, R, D), bf16),
-        "XRA": ((4, A // 4, RB, D), bf16),
-        "YRA": ((4, A - A // 4, RB, D // 2), bf16),
-        "YRB": ((4, A // 4, 2, RB, D // 2), bf16),
-        "XRB": ((4, A // 4, RB, D // 2), bf16),
+        "YRA": ((4, A // 2, RB, D // 2), bf16),
+        "YRB": ((4, A // 2, 2, RB, D // 2), bf16),
+        "XRB": ((4, A // 2, RB, D // 2), bf16),
         "ZR": ((4, A - 1, RB, D // 2), bf16),
         "FINA": ((4, 2, RB, D), bf16),
         "COLS": ((T, LANES), f32),

time: 264 us -> 249 us (0.943)
  Pallas kernels: 258 us -> 245 us
    pallas_call x1, Pallas kernels: 242 us -> 228 us  [run_block(): pl.pallas_call(functools.partial(block_kernel, dims, names), out_shape=[j...]
where the time goes in v5:
time: 249 us; the launch traced here: 248 us
  Pallas kernels  245 us (98%)
  other arithmetic  2.62 us (1%)
    pallas_call x1, Pallas kernels, run_block(): pl.pallas_call(functools.partial(block_kernel, dims, names), out_shape=[j...  228 us
    pallas_call x1, Pallas kernels, finish(): pl.pallas_call(kernel, grid=(S * per,), out_shape=[shape(block_input.shap...  16.4 us

profile of v5, /device:TPU:0, one launch (start us, length us, event | category | flops | bytes accessed | tf_op | source)
XLA Modules:
  0.0 248.2 jit_solution(11433569667267909706)
XLA Ops:
  0.7 0.7 convert_element_type.6
  1.3 0.7 broadcast_select_fusion
  2.0 1.2 convert_dynamic-update-slice_fusion.refs_8_
  3.3 228.4 %routed_block.1 = (bf16[512,1024]{1,0:T(8,128)(2,1)}, bf16[512,1024]{1,0:T(8,128)(2,1)}, bf16[2,4,128,1024]{3,2,1,0:T(8,128)(2,1)}, bf16[4,2,64,1024]{3,2,1,0:T(8,128)(2,1)}, f32[8,1024]{1,0:T(8,128)}) custom-call(bf16[2,2048,1024]{2,1,0:T(8,128)(2,1)} %base.1, bf16[2,2048,1024]{2,1,0:T(8,128)(2,1)} %base_grad.1, bf16[128,1024]{1,0:T(8,128)(2,1)} %refs_2_.1, ...), custom_call_target="tpu_custom_call" | custom-call | tf_op jit(solution)/shard_map/routed_block/pallas_call | solution.py:1042
  231.7 16.4 %finish_rows.1 = (bf16[2,2048,1024]{2,1,0:T(8,128)(2,1)}, bf16[2,2048,1024]{2,1,0:T(8,128)(2,1)}, f32[1,2]{1,0:T(1,128)}, f32[1,1024]{1,0:T(1,128)}, f32[1,128]{...) custom-call(s32[2,256]{1,0:T(2,128)} %slots.1, ...), custom_call_target="tpu_custom_call" | custom-call | tf_op jit(solution)/shard_map/finish_rows/pallas_call | solution.py:959
  (1 shorter events, 0.0 us)

commit v6 on v5

--- a/solution.py
+++ b/solution.py
@@ -85,7 +85,7 @@
 
 def copy_count(far):
     near = far - 1
-    gather = 4 * (8 * near + 2) + 5 * (2 * near + 1)
+    gather = 4 * (8 * near + 2) + 7 * (2 * near + 1)
     narrow = 2 * 6 + 2 * 4
     reduce_mlp = 2 * (far + near + 3)
     reduce_attn = 4 * (1 + 2 * far + near + 3)
@@ -238,10 +238,13 @@
     gains = WideGather(lambda zz, xx: GP.at[zz * 2 + xx])
     query, key, value, out = (AttnGather(g, 1) for g in range(4))
     attn = (query, key, value, out)
-    up, down = (
-        [WideGather(lambda zz, xx, ref=ref, h=h: ref.at[zz, xx, pl.ds(h * RB, RB)]) for h in range(2)]
-        for ref in (WU, WD)
-    )
+    def in_parts(ref, count):
+        size = R // count
+        return [
+            WideGather(lambda zz, xx, h=h: ref.at[zz, xx, pl.ds(h * size, size)]) for h in range(count)
+        ]
+
+    up, down = in_parts(WU, 2), in_parts(WD, 4 if R % 64 == 0 else 2)
     gains.start()
     gains.start_near()
     for group in attn:
@@ -449,8 +452,9 @@
     project_out(1)
     norm_two(1)
     share_nt.start(1)
-    for dz in far:
-        down[0].relay(dz)
+    for part in down[: len(down) // 2]:
+        for dz in far:
+            part.relay(dz)
 
     tanh_k = math.sqrt(2.0 / math.pi)
 
@@ -489,8 +493,9 @@
     for part in up:
         part.finish()
     up_unit(y, 0)
-    for dz in far:
-        down[1].relay(dz)
+    for part in down[len(down) // 2 :]:
+        for dz in far:
+            part.relay(dz)
     up_unit(y, 1)
     share_nt.relay(0)
     share_nt.last[0].wait_recv()

time: 249 us -> 249 us (level)
  no operation moved by 1% of the time
where the time goes in v6:
time: 249 us
  Pallas kernels  245 us (98%)
  other arithmetic  2.62 us (1%)
    pallas_call x1, Pallas kernels, run_block(): pl.pallas_call(functools.partial(block_kernel, dims, names), out_shape=[j...  229 us
    pallas_call x1, Pallas kernels, finish(): pl.pallas_call(kernel, grid=(S * per,), out_shape=[shape(block_input.shap...  16.4 us

profile of v6, /device:TPU:0, one launch (start us, length us, event | category | flops | bytes accessed | tf_op | source)
XLA Modules:
  0.0 248.5 jit_solution(16688786705383992688)
XLA Ops:
  0.7 0.7 convert_element_type.6
  1.3 0.7 broadcast_select_fusion
  2.0 1.2 convert_dynamic-update-slice_fusion.refs_8_
  3.3 228.7 %routed_block.1 = (bf16[512,1024]{1,0:T(8,128)(2,1)}, bf16[512,1024]{1,0:T(8,128)(2,1)}, bf16[2,4,128,1024]{3,2,1,0:T(8,128)(2,1)}, bf16[4,2,64,1024]{3,2,1,0:T(8,128)(2,1)}, f32[8,1024]{1,0:T(8,128)}) custom-call(bf16[2,2048,1024]{2,1,0:T(8,128)(2,1)} %base.1, bf16[2,2048,1024]{2,1,0:T(8,128)(2,1)} %base_grad.1, bf16[128,1024]{1,0:T(8,128)(2,1)} %refs_2_.1, ...), custom_call_target="tpu_custom_call" | custom-call | tf_op jit(solution)/shard_map/routed_block/pallas_call | solution.py:1047
  232.0 16.4 %finish_rows.1 = (bf16[2,2048,1024]{2,1,0:T(8,128)(2,1)}, bf16[2,2048,1024]{2,1,0:T(8,128)(2,1)}, f32[1,2]{1,0:T(1,128)}, f32[1,1024]{1,0:T(1,128)}, f32[1,128]{...) custom-call(s32[2,256]{1,0:T(2,128)} %slots.1, ...), custom_call_target="tpu_custom_call" | custom-call | tf_op jit(solution)/shard_map/finish_rows/pallas_call | solution.py:964
  (1 shorter events, 0.0 us)
